TPU v7x, 32 devices: a whole 2x2x4 slice. The times are simulated.
32 devices in a mesh: dp: 8 (over z, y), shard: 4 (over x, core).
Axes of the slice: x: 2, y: 2, z: 4, core: 2. Of those that a mesh axis runs over, the one named last changes fastest.
Arguments:
- key_grad: bfloat16 [8, 512, 2560], P('dp', 'shard'), may hold values from -90 to 90
- key_error: float32 [8, 512, 2560], P('dp', 'shard'), may hold values from -4 to 4
- router_grad: bfloat16 [8, 64, 2560], P('dp', 'shard'), may hold values from -90 to 90
- router_error: float32 [8, 64, 2560], P('dp', 'shard'), may hold values from -4 to 4
- norm_grad: bfloat16 [8, 2, 2560], P('dp', None, 'shard'), may hold values from -8 to 8
- key_basis: float32 [32, 2560], replicated, may hold values from -6 to 6
- router_basis: float32 [32, 2560], replicated, may hold values from -6 to 6
- key_momentum: float32 [512, 2560], P('shard', 'dp'), may hold values from -4 to 4
- key_weight: float32 [512, 2560], P('shard', 'dp'), may hold values from -4 to 4
- router_momentum: float32 [64, 2560], P('shard', 'dp'), may hold values from -4 to 4
- router_weight: float32 [64, 2560], P('shard', 'dp'), may hold values from -4 to 4
- norm_momentum: float32 [2, 2560], P(None, 'shard'), may hold values from -4 to 4
- norm_weight: float32 [2, 2560], P(None, 'shard'), may hold values from 0.5 to 1.5
Outputs:
- key_carry: float32 [8, 512, 2560], P('dp', 'shard')
- router_carry: float32 [8, 64, 2560], P('dp', 'shard')
- key_velocity: float32 [512, 2560], P('shard', 'dp')
- key_master: float32 [512, 2560], P('shard', 'dp')
- key_params: bfloat16 [512, 2560], P(None, 'dp')
- router_velocity: float32 [64, 2560], P('shard', 'dp')
- router_master: float32 [64, 2560], P('shard', 'dp')
- router_params: bfloat16 [64, 2560], P(None, 'dp')
- norm_velocity: float32 [2, 2560], P(None, 'shard')
- norm_master: float32 [2, 2560], P(None, 'shard')
- norm_params: bfloat16 [2, 2560], replicated
All inputs are finite; a program needn't handle non-finite values.
Results may differ from a plain program's by a relative error of at most 0.008.
Values may be sent and summed in bfloat16 or wider, within the bound.
A program may use at most 64 MiB of HBM per device.

v0:
```python
import jax
import jax.numpy as jnp
from jax import lax
from jax.sharding import PartitionSpec as P

ROOT_STEPS = 4


highest = lax.Precision.HIGHEST
momentum_decay = 0.9
learning_rate = 0.1


def inverse_root(gram_matrix):
    scaling = jnp.sqrt(jnp.sum(gram_matrix * gram_matrix)) + 1e-06
    identity = jnp.eye(gram_matrix.shape[0], dtype=jnp.float32)
    square_side = gram_matrix / scaling
    root_side = identity
    for sweep_index in range(ROOT_STEPS):
        middle = 1.5 * identity - 0.5 * jnp.dot(root_side, square_side, precision=highest)
        square_side = jnp.dot(square_side, middle, precision=highest)
        root_side = jnp.dot(middle, root_side, precision=highest)
    return (root_side, scaling)


def project(old_basis, merged):
    return lax.dot_general(old_basis, merged, (((1,), (1,)), ((), ())), precision=highest)


def gram_of(factor_rows):
    return lax.dot_general(factor_rows, factor_rows, (((1,), (1,)), ((), ())), precision=highest)


def normalize(gram_matrix, factor_rows):
    root_side, scaling = inverse_root(gram_matrix)
    return jnp.dot(root_side, factor_rows, precision=highest) / jnp.sqrt(scaling)


def advance(momentum, weight, direction):
    velocity = momentum_decay * momentum + direction
    return (velocity, weight - learning_rate * velocity)


def body(
    key_grad,
    key_error,
    router_grad,
    router_error,
    norm_grad,
    key_basis,
    router_basis,
    key_momentum,
    key_weight,
    router_momentum,
    router_weight,
    norm_momentum,
    norm_weight,
):
    replicas = lax.axis_size("dp")
    rank_size = key_basis.shape[0]
    merged_key = key_grad[0].astype(jnp.float32) + key_error[0]
    merged_router = router_grad[0].astype(jnp.float32) + router_error[0]
    rows_key, rows_router, norm_sum = lax.psum(
        (
            project(key_basis, merged_key),
            project(router_basis, merged_router),
            norm_grad[0].astype(jnp.float32),
        ),
        "dp",
    )
    gram_key, gram_router = lax.psum((gram_of(rows_key), gram_of(rows_router)), "shard")
    ortho_key = normalize(gram_key, rows_key)
    ortho_router = normalize(gram_router, rows_router)
    key_part = lax.dot_general(merged_key, ortho_key, (((0,), (1,)), ((), ())), precision=highest)
    router_part = lax.dot_general(
        merged_router, ortho_router, (((0,), (1,)), ((), ())), precision=highest
    )
    column_sum = lax.psum(jnp.concatenate([key_part, router_part], axis=1), ("dp", "shard"))
    columns = column_sum / replicas
    approx_key = lax.dot_general(
        ortho_key, columns[:, :rank_size], (((0,), (1,)), ((), ())), precision=highest
    )
    approx_router = lax.dot_general(
        ortho_router, columns[:, rank_size:], (((0,), (1,)), ((), ())), precision=highest
    )
    col_width = key_momentum.shape[1]
    offset = lax.axis_index("dp") * col_width
    key_velocity, key_master = advance(
        key_momentum, key_weight, lax.dynamic_slice_in_dim(approx_key, offset, col_width, 1)
    )
    router_velocity, router_master = advance(
        router_momentum,
        router_weight,
        lax.dynamic_slice_in_dim(approx_router, offset, col_width, 1),
    )
    norm_velocity, norm_master = advance(norm_momentum, norm_weight, norm_sum / replicas)
    key_params, router_params, norm_params = (
        lax.all_gather(key_master.astype(jnp.bfloat16), "shard", axis=0, tiled=True),
        lax.all_gather(router_master.astype(jnp.bfloat16), "shard", axis=0, tiled=True),
        lax.all_gather(norm_master.astype(jnp.bfloat16), "shard", axis=1, tiled=True),
    )
    key_carry = (merged_key - approx_key)[None]
    router_carry = (merged_router - approx_router)[None]
    return (
        key_carry,
        router_carry,
        key_velocity,
        key_master,
        key_params,
        router_velocity,
        router_master,
        router_params,
        norm_velocity,
        norm_master,
        norm_params,
    )


def solution(mesh):
    return jax.shard_map(
        body,
        mesh=mesh,
        in_specs=(
            P("dp", "shard", None),
            P("dp", "shard", None),
            P("dp", "shard", None),
            P("dp", "shard", None),
            P("dp", None, "shard"),
            P(),
            P(),
            P("shard", "dp"),
            P("shard", "dp"),
            P("shard", "dp"),
            P("shard", "dp"),
            P(None, "shard"),
            P(None, "shard"),
        ),
        out_specs=(
            P("dp", "shard", None),
            P("dp", "shard", None),
            P("shard", "dp"),
            P("shard", "dp"),
            P(None, "dp"),
            P("shard", "dp"),
            P("shard", "dp"),
            P(None, "dp"),
            P(None, "shard"),
            P(None, "shard"),
            P(),
        ),
        check_vma=False,
    )
```

profile of v0, /device:TPU:0, one launch (start us, length us, event | category | flops | bytes accessed | tf_op | source)
XLA Modules:
  0.0 224.1 jit_solution(4656349476250035121)
XLA Ops:
  7.2 0.7 bitcast_convert_fusion
  8.0 1.4 convolution_bitcast_fusion
  9.5 2.9 %fusion.5 = f32[32,128]{1,0:T(8,128)S(1)} fusion(f32[32,2560]{1,0:T(8,128)S(1)} %copy-done, f32[1,128,2560]{2,1,0:T(8,128)} %param.14, bf16[1,128,2560]{2,1,0:T(8,128)(2,1)} %param.13), kind=kOutput, calls=%fused_computation.7 | convolution fusion | flops 126484480 | bytes 2310144 | tf_op jit(solution)/shard_map/dot_general | solution.py:27
  12.4 38.9 %all-reduce = (f32[32,128]{1,0:T(8,128)S(1)}, f32[32,16]{0,1:T(8,128)S(1)}, f32[2,640]{1,0:T(2,128)S(1)}) all-reduce(f32[32,128]{1,0:T(8,128)S(1)} %fusion.5, f32[32,16]{0,1:T(8,128)S(1)} %convolution_bitcast_fusion, f32[2,640]{1,0:T(2,128)S(1)} %bitcast_convert_fusion), channel_id=1, replica_groups=mesh['dp'=8,'shard'=4] {'dp'}, use_global_device_ids=true, to_apply=%region_0.0 | all-reduce | flops 5888 | bytes 47104 | tf_op jit(solution)/shard_map/psum | solution.py:63
  51.3 0.1 fusion.31
  51.4 0.2 fusion.37
  51.6 10.3 %all-reduce.1 = (f32[32,32]{1,0:T(8,128)S(1)}, f32[32,32]{1,0:T(8,128)S(1)}) all-reduce(f32[32,32]{1,0:T(8,128)S(1)} %fusion.31, f32[32,32]{1,0:T(8,128)S(1)} %fusion.37), channel_id=1, replica_groups=mesh['dp'=8,'shard'=4] {'shard'}, use_global_device_ids=true, to_apply=%region_1.0 | all-reduce | flops 2048 | bytes 16384 | tf_op jit(solution)/shard_map/psum | solution.py:71
  61.9 0.6 multiply_reduce_fusion
  63.3 0.1 fusion.11
  63.4 0.1 fusion.27
  63.6 0.1 fusion.24
  63.7 0.2 fusion.10
  63.9 0.1 fusion.39
  64.0 0.1 fusion.38
  64.1 0.2 fusion.9
  64.3 0.1 fusion.40
  64.4 0.1 fusion.41
  65.4 0.1 fusion.15
  65.5 0.2 fusion.26
  65.8 0.2 fusion.14
  65.9 0.1 fusion.33
  66.1 0.1 fusion.32
  66.2 0.2 fusion.13
  66.4 0.1 fusion.34
  66.7 0.2 fusion.8
  67.0 0.2 fusion.12
  67.2 0.2 fusion.36
  67.3 0.2 convolution_divide_fusion
  67.5 0.9 fusion
  68.4 0.1 convolution_divide_fusion.1
  68.6 0.5 fusion.20
  69.1 0.9 pad_maximum_fusion
  70.0 0.6 fusion.28
  70.6 5.1 %all_gather.11 = bf16[2,2560]{1,0:T(2,128)(2,1)S(1)} all-gather(bf16[2,640]{1,0:T(2,128)(2,1)S(1)} %get-tuple-element.27), channel_id=1, replica_groups=mesh['dp'=8,'shard'=4] {'shard'}, dimensions={1}, use_global_device_ids=true | all-gather | bytes 12800 | tf_op jit(solution)/shard_map/all_gather | solution.py:100
  76.0 120.2 %all-reduce.4.cloned.1.call-done = f32[2560,64]{0,1:T(8,128)} async-done(((f32[2560,64]{0,1:T(8,128)}), f32[2560,64]{0,1:T(8,128)}) %all-reduce.4.cloned.1.call-update) | async-done | bytes 655376 | tf_op jit(solution)/shard_map/psum | solution.py:78
  196.2 1.1 broadcast_multiply_fusion
  197.4 0.3 fusion.16
  197.7 1.2 fusion.18
  198.9 0.7 fusion.23
  199.6 0.7 fusion.29
  200.3 5.2 %all_gather.10 = bf16[64,320]{1,0:T(8,128)(2,1)S(1)} all-gather(bf16[16,320]{1,0:T(8,128)(2,1)S(1)} %get-tuple-element.30), channel_id=1, replica_groups=mesh['dp'=8,'shard'=4] {'shard'}, dimensions={0}, use_global_device_ids=true | all-gather | bytes 51200 | tf_op jit(solution)/shard_map/all_gather | solution.py:99
  205.5 1.3 fusion.4
  207.0 0.8 copy.27
  207.8 0.8 copy.26
  208.5 6.5 %all_gather.9 = bf16[512,320]{1,0:T(8,128)(2,1)S(1)} all-gather(bf16[128,320]{1,0:T(8,128)(2,1)S(1)} %get-tuple-element.33), channel_id=1, replica_groups=mesh['dp'=8,'shard'=4] {'shard'}, dimensions={0}, use_global_device_ids=true | all-gather | bytes 409600 | tf_op jit(solution)/shard_map/all_gather | solution.py:98
  215.1 0.9 copy.28
  216.0 0.6 copy.32
  216.6 0.6 copy.33
  (30 shorter events, 0.9 us)
Async XLA Ops:
  7.2 2.3 %copy-start = (f32[32,2560]{1,0:T(8,128)S(1)}, f32[32,2560]{1,0:T(8,128)}, u32[]{:S(2)}) copy-start(f32[32,2560]{1,0:T(8,128)} %param.18) | copy-start | bytes 983044
  7.2 189.0 %all-reduce.4.cloned.1.call-start = ((), (), s32[]{:S(2)}) async-start(), calls=%async_computation | async-start | bytes 1310720 | tf_op jit(solution)/shard_map/psum | solution.py:78
  9.4 58.0 %copy-start.1 = (f32[1,128,2560]{2,1,0:T(8,128)S(1)}, f32[1,128,2560]{2,1,0:T(8,128)}, u32[]{:S(2)}) copy-start(f32[1,128,2560]{2,1,0:T(8,128)} %param.14) | copy-start | bytes 3932164
  9.5 58.0 %copy-start.2 = (bf16[1,128,2560]{2,1,0:T(8,128)(2,1)S(1)}, bf16[1,128,2560]{2,1,0:T(8,128)(2,1)}, u32[]{:S(2)}) copy-start(bf16[1,128,2560]{2,1,0:T(8,128)(2,1)} %param.13) | copy-start | bytes 1966084
  66.5 2.0 copy-start.3
  66.6 2.0 copy-start.4
  68.4 1.6 copy-start.9
  68.4 1.6 copy-start.10
  68.6 7.2 %copy-start.5 = (f32[128,320]{0,1:T(8,128)S(1)}, f32[128,320]{0,1:T(8,128)}, u32[]{:S(2)}) copy-start(f32[128,320]{0,1:T(8,128)} %param.20) | copy-start | bytes 491524
  69.1 6.8 %copy-start.6 = (f32[128,320]{0,1:T(8,128)S(1)}, f32[128,320]{0,1:T(8,128)}, u32[]{:S(2)}) copy-start(f32[128,320]{0,1:T(8,128)} %param.21) | copy-start | bytes 491524
  197.4 2.3 %copy-start.7 = (f32[16,320]{1,0:T(8,128)S(1)}, f32[16,320]{1,0:T(8,128)}, u32[]{:S(2)}) copy-start(f32[16,320]{1,0:T(8,128)} %param.23) | copy-start | bytes 61444
  197.4 2.2 %copy-start.8 = (f32[16,320]{1,0:T(8,128)S(1)}, f32[16,320]{1,0:T(8,128)}, u32[]{:S(2)}) copy-start(f32[16,320]{1,0:T(8,128)} %param.22) | copy-start | bytes 61444
Sparse Core Ops, SparseCore 0:
  70.1 126.0 all-reduce.3
where the time goes:
time: 224 us
  waiting for transfers between devices  120 us (54%)
  blocking collectives  66.1 us (30%)
  between operations  15.8 us (7%)
  matrix products  11.1 us (5%)
  other arithmetic  6.77 us (3%)
  local copies, waits for them, and re-layouts  4.05 us (2%)
    psum x1, waiting for transfers between devices, body(): lax.psum(jnp.concatenate([key_part, router_part], axis=1), ('dp', 'shard'))  120 us
    psum x1, blocking collectives, body(): lax.psum((project(key_basis, merged_key), project(router_basis, merged_ro...  38.9 us
    psum x1, blocking collectives, body(): lax.psum((gram_of(rows_key), gram_of(rows_router)), 'shard')  10.3 us
    all_gather x1, blocking collectives, body(): lax.all_gather(key_master.astype(jnp.bfloat16), 'shard', axis=0, tiled=True)  6.55 us
    all_gather x1, blocking collectives, body(): lax.all_gather(router_master.astype(jnp.bfloat16), 'shard', axis=0, tiled...  5.21 us
    all_gather x1, blocking collectives, body(): lax.all_gather(norm_master.astype(jnp.bfloat16), 'shard', axis=1, tiled=T...  5.15 us
  transfers between devices with their start and end apart: 1, of which 1 were waited for; matrix products, arithmetic and copies ran while one was open for 0% of the time, Pallas kernels for 0%

commit v1 on v0

--- a/solution.py
+++ b/solution.py
@@ -1,14 +1,21 @@
+import functools
+
 import jax
 import jax.numpy as jnp
 from jax import lax
+from jax.experimental import pallas as pl
+from jax.experimental.pallas import tpu as pltpu
 from jax.sharding import PartitionSpec as P
 
 ROOT_STEPS = 4
-
+MESH = pl.DeviceIdType.MESH
+LANES = 128
 
 highest = lax.Precision.HIGHEST
 momentum_decay = 0.9
 learning_rate = 0.1
+f32 = jnp.float32
+bf16 = jnp.bfloat16
 
 
 def inverse_root(gram_matrix):
@@ -41,7 +48,7 @@
     return (velocity, weight - learning_rate * velocity)
 
 
-def body(
+def general_body(
     key_grad,
     key_error,
     router_grad,
@@ -116,7 +123,384 @@
     )
 
 
+def halves(x):
+    high = x.astype(bf16)
+    return high, (x - high.astype(f32)).astype(bf16)
+
+
+def fold(x, rows, cols):
+    y = x[:rows] + x[rows:]
+    return y[:, :cols] + y[:, cols:]
+
+
+def window(d):
+    return (5 * d // 2) * LANES
+
+
+def packed(x):
+    pieces = [x[:, LANES * j : LANES * (j + 1)] for j in range(x.shape[1] // LANES)]
+    rows = 2 * len(pieces)
+    return jnp.concatenate(pieces + [jnp.zeros((16 - rows, LANES), f32)], axis=0)
+
+
+def exchange_kernel(
+    n_dp, n_shard, rank,
+    kg, ke, rg, re, ng, kb, rb, km, kw, rm, rw, nm, nw,
+    ortho, cols, ufull, nsum, npar,
+    mk, mr, p64, recv1, recv2, nsend, nrecv, csend, crecv, bsend, brecv, send, recv,
+):
+    d = lax.axis_index("dp")
+    s = lax.axis_index("shard")
+    total = n_dp * n_shard
+    me = d * n_shard + s
+    core = lax.rem(s, 2)
+    x = s // 2
+    mate = s + 1 - 2 * core
+    half = total // 2
+    q = x * n_dp + d
+    key_rows, width = mk.shape[0] // 2, mk.shape[1]
+    router_rows = mr.shape[0] // 2
+
+    def peer_all(j):
+        t = lax.rem(me + j, total)
+        return (t // n_shard, lax.rem(t, n_shard))
+
+    barrier = pltpu.get_barrier_semaphore()
+
+    def greet(j, carry):
+        pl.semaphore_signal(barrier, inc=1, device_id=peer_all(j), device_id_type=MESH)
+        return carry
+
+    lax.fori_loop(1, total, greet, 0)
+
+    def put(src, dst, which, device):
+        pltpu.make_async_remote_copy(
+            src_ref=src, dst_ref=dst, send_sem=send.at[which], recv_sem=recv.at[which],
+            device_id=device, device_id_type=MESH,
+        ).start()
+
+    def wait_recv(ref, which):
+        pltpu.make_async_copy(ref, ref, recv.at[which]).wait()
+
+    def wait_send(ref, which):
+        pltpu.make_async_copy(ref, ref, send.at[which]).wait()
+
+    high, low = halves(kg[0].astype(f32) + ke[0])
+    mk[:key_rows] = high
+    mk[key_rows:] = low
+    high, low = halves(rg[0].astype(f32) + re[0])
+    mr[:router_rows] = high
+    mr[router_rows:] = low
+    nt = (((1,), (1,)), ((), ()))
+    kb2 = jnp.concatenate(halves(kb[...]), axis=0)
+    pk = lax.dot_general(kb2, mk[...], nt, preferred_element_type=f32)
+    p64[:rank] = fold(pk, rank, key_rows)
+    rb2 = jnp.concatenate(halves(rb[...]), axis=0)
+    pr = lax.dot_general(rb2, mr[...], nt, preferred_element_type=f32)
+    p64[rank:] = jnp.concatenate(
+        [fold(pr, rank, router_rows), jnp.zeros((rank, LANES - router_rows), f32)], axis=1
+    )
+    nsend[0] = packed(ng[0].astype(f32)).astype(bf16)
+
+    pl.semaphore_wait(barrier, total - 1)
+
+    def send_rows(j, carry):
+        t = lax.rem(d + j, n_dp)
+        put(p64.at[pl.ds(pl.multiple_of(t * 8, 8), 8)], recv1.at[d], 0, (t, s))
+        return carry
+
+    lax.fori_loop(1, n_dp, send_rows, 0)
+
+    def send_norm(j, carry):
+        t = lax.rem(d + j, n_dp)
+        put(nsend.at[0], nrecv.at[d], 1, (t, s))
+        return carry
+
+    lax.fori_loop(1, n_dp, send_norm, 0)
+    recv1[d] = p64[pl.ds(pl.multiple_of(d * 8, 8), 8), :]
+    nrecv[d] = nsend[0]
+    wait_recv(recv1.at[pl.ds(0, n_dp - 1)], 0)
+    slot = s * n_dp + d
+    recv2[slot] = jnp.sum(recv1[...], axis=0)
+
+    def send_sum(j, carry):
+        put(recv2.at[slot], recv2.at[slot], 2, peer_all(j))
+        return carry
+
+    lax.fori_loop(1, total, send_sum, 0)
+
+    decay = learning_rate * momentum_decay
+    ufull[s, :key_rows] = (kw[...] - decay * km[...]).astype(bf16)
+    ufull[s, key_rows:] = (rw[...] - decay * rm[...]).astype(bf16)
+    for j in range(1, n_shard):
+        put(ufull.at[s], ufull.at[s], 3, (d, lax.rem(s + j, n_shard)))
+
+    wait_recv(nrecv.at[pl.ds(0, n_dp - 1)], 1)
+    norm_sum = jnp.sum(nrecv[...].astype(f32), axis=0)
+    nsum[...] = norm_sum
+    norm_velocity, norm_master = advance(packed(nm[...]), packed(nw[...]), norm_sum / n_dp)
+    npar[s] = norm_master.astype(bf16)
+    for j in range(1, n_shard):
+        put(npar.at[s], npar.at[s], 4, (d, lax.rem(s + j, n_shard)))
+
+    wait_recv(recv2.at[pl.ds(0, total - 1)], 2)
+
+    both = 2 * rank
+    rows = jnp.concatenate(
+        [recv2[n_dp * k : n_dp * (k + 1)].reshape(both, LANES) for k in range(n_shard)], axis=1
+    )
+    down = lax.broadcasted_iota(jnp.int32, (both, both), 0)
+    along = lax.broadcasted_iota(jnp.int32, (both, both), 1)
+    gram = lax.dot_general(rows, rows, nt, precision=highest, preferred_element_type=f32)
+    gram = jnp.where((down < rank) == (along < rank), gram, 0.0)
+    identity = jnp.where(down == along, 1.0, 0.0).astype(f32)
+    square = gram * gram
+    scale_key = jnp.sqrt(jnp.sum(square[:rank], keepdims=True)) + 1e-06
+    scale_router = jnp.sqrt(jnp.sum(square[rank:], keepdims=True)) + 1e-06
+    row_index = lax.broadcasted_iota(jnp.int32, (both, 1), 0)
+    scaling = jnp.where(row_index < rank, scale_key, scale_router)
+
+    def mul(a, b):
+        return jnp.dot(a, b, precision=highest, preferred_element_type=f32)
+
+    t = gram / scaling
+    middle = 1.5 * identity - 0.5 * t
+    root = middle
+    for step in range(1, ROOT_STEPS):
+        t = mul(t, 2.25 * identity - 1.5 * t + 0.25 * mul(t, t))
+        middle = 1.5 * identity - 0.5 * t
+        if step < ROOT_STEPS - 1:
+            root = mul(middle, root)
+    ortho[...] = mul(middle, mul(root, rows)) / jnp.sqrt(scaling)
+
+    own = ortho[:, pl.ds(pl.multiple_of(s * LANES, LANES), LANES)]
+
+    def columns_of(factor, merged):
+        high, low = halves(factor)
+        left = jnp.concatenate(
+            [jnp.concatenate([high, high], axis=1), jnp.concatenate([low, low], axis=1)], axis=0
+        )
+        out = jnp.dot(left, merged, preferred_element_type=f32)
+        return out[:rank] + out[rank:]
+
+    part_key = columns_of(own[:rank], mk[...]).astype(bf16)
+    part_router = columns_of(own[rank:, :router_rows], mr[...]).astype(bf16)
+    for k in range(n_shard):
+        part = part_key if k < n_shard // 2 else part_router
+        top = 16 * (k % (n_shard // 2))
+        for b in range(n_dp):
+            at = (k % 2) * half + (k // 2) * n_dp + b
+            csend[at] = part[top : top + 16, window(b) : window(b) + 3 * LANES]
+
+    there = csend.at[pl.ds((1 - core) * half, half)]
+    put(there, crecv, 5, (d, mate))
+    wait_recv(crecv, 5)
+    bsend[...] = (csend[pl.ds(core * half, half)].astype(f32) + crecv[...].astype(f32)).astype(bf16)
+
+    def peer_core(j):
+        to = lax.rem(q + j, half)
+        return to, (lax.rem(to, n_dp), (to // n_dp) * 2 + core)
+
+    def send_part(j, carry):
+        to, device = peer_core(j)
+        put(bsend.at[to], brecv.at[q], 6, device)
+        return carry
+
+    lax.fori_loop(1, half, send_part, 0)
+    brecv[q] = bsend[q]
+    wait_recv(brecv.at[pl.ds(0, half - 1)], 6)
+    mine = core * half + q
+    cols[mine] = (jnp.sum(brecv[...].astype(f32), axis=0) / n_dp).astype(bf16)
+
+    def send_columns(j, carry):
+        to, device = peer_core(j)
+        put(cols.at[mine], cols.at[mine], 7, device)
+        return carry
+
+    lax.fori_loop(1, half, send_columns, 0)
+    wait_recv(cols.at[pl.ds(0, half - 1)], 7)
+    ours = cols.at[pl.ds(core * half, half)]
+    put(ours, ours, 8, (d, mate))
+
+    wait_recv(ufull.at[pl.ds(0, n_shard - 1)], 3)
+    wait_recv(npar.at[pl.ds(0, n_shard - 1)], 4)
+    wait_send(recv1.at[pl.ds(0, n_dp - 1)], 0)
+    wait_send(nrecv.at[pl.ds(0, n_dp - 1)], 1)
+    wait_send(recv2.at[pl.ds(0, total - 1)], 2)
+    wait_send(ufull.at[pl.ds(0, n_shard - 1)], 3)
+    wait_send(npar.at[pl.ds(0, n_shard - 1)], 4)
+    wait_send(crecv, 5)
+    wait_send(brecv.at[pl.ds(0, half - 1)], 6)
+    wait_send(cols.at[pl.ds(0, half - 1)], 7)
+    wait_recv(ours, 8)
+    wait_send(ours, 8)
+
+
+def finish_kernel(
+    n_dp, n_shard, rank,
+    kg, ke, rg, re, km, kw, rm, rw, nm, nw, ortho, cols, ufull, nsum, npar,
+    key_carry, router_carry, key_velocity, key_master, key_params,
+    router_velocity, router_master, router_params, norm_velocity, norm_master, norm_params,
+    ck, cr,
+):
+    d = lax.axis_index("dp")
+    s = lax.axis_index("shard")
+    half = n_dp * n_shard // 2
+    key_rows, router_rows = kg.shape[1], rg.shape[1]
+    span = km.shape[1]
+    for k in range(n_shard):
+        where = ck if k < n_shard // 2 else cr
+        top = 16 * (k % (n_shard // 2))
+        for b in range(n_dp):
+            at = (k % 2) * half + (k // 2) * n_dp + b
+            skip = LANES if b % 2 else 0
+            piece = cols[at][:, skip:]
+            lane = window(b) + skip
+            where[top : top + 16, lane : window(b) + 3 * LANES] = piece
+            where[rank + top : rank + top + 16, lane : window(b) + 3 * LANES] = piece
+
+    def turned(factor):
+        return jnp.concatenate(halves(factor.T), axis=1)
+
+    def dot(a, b):
+        return jnp.dot(a, b, preferred_element_type=f32)
+
+    own = ortho[:, pl.ds(pl.multiple_of(s * LANES, LANES), LANES)]
+    own_key = turned(own[:rank])
+    own_router = turned(own[rank:])[:router_rows]
+    key_carry[0] = kg[0].astype(f32) + ke[0] - dot(own_key, ck[...])
+    router_carry[0] = rg[0].astype(f32) + re[0] - dot(own_router, cr[...])
+
+    def block(first):
+        parts = []
+        for k in (first, first + 1):
+            parts.append(cols[(k % 2) * half + (k // 2) * n_dp + d].astype(f32))
+        both = jnp.concatenate(parts, axis=0)
+        extra = both.shape[1] - span
+        picked = jnp.where(lax.rem(d, 2) == 1, both[:, extra:], both[:, :span]).astype(bf16)
+        return jnp.concatenate([picked, picked], axis=0)
+
+    block_key = block(0)
+    block_router = block(n_shard // 2)
+    key_velocity[...], key_master[...] = advance(km[...], kw[...], dot(own_key, block_key))
+    router_velocity[...], router_master[...] = advance(
+        rm[...], rw[...], dot(own_router, block_router)
+    )
+    for k in range(n_shard):
+        factor = ortho[:, LANES * k : LANES * (k + 1)]
+        approx = dot(turned(factor[:rank]), block_key)
+        held = ufull[k].astype(f32)
+        key_params[key_rows * k : key_rows * (k + 1)] = (
+            held[:key_rows] - learning_rate * approx
+        ).astype(bf16)
+        approx = dot(turned(factor[rank:])[:router_rows], block_router)
+        router_params[router_rows * k : router_rows * (k + 1)] = (
+            held[key_rows:] - learning_rate * approx
+        ).astype(bf16)
+
+    pieces = nm.shape[1] // LANES
+
+    def unpacked(x):
+        return jnp.concatenate([x[2 * j : 2 * j + 2] for j in range(pieces)], axis=1)
+
+    norm_velocity[...], norm_master[...] = advance(nm[...], nw[...], unpacked(nsum[...]) / n_dp)
+    norm_params[...] = jnp.concatenate(
+        [unpacked(npar[k].astype(f32)) for k in range(n_shard)], axis=1
+    ).astype(bf16)
+
+
+def fast_body(
+    n_dp, n_shard,
+    key_grad, key_error, router_grad, router_error, norm_grad, key_basis, router_basis,
+    key_momentum, key_weight, router_momentum, router_weight, norm_momentum, norm_weight,
+):
+    rank, width = key_basis.shape
+    key_rows, router_rows = key_grad.shape[1], router_grad.shape[1]
+    span = key_momentum.shape[1]
+    total, half = n_dp * n_shard, n_dp * n_shard // 2
+    vmem = pl.BlockSpec(memory_space=pltpu.VMEM)
+    shape = jax.ShapeDtypeStruct
+    chunk = (16, 3 * LANES)
+    middle = pl.pallas_call(
+        functools.partial(exchange_kernel, n_dp, n_shard, rank),
+        out_shape=[
+            shape((2 * rank, n_shard * LANES), f32),
+            shape((total,) + chunk, bf16),
+            shape((n_shard, key_rows + router_rows, span), bf16),
+            shape((16, LANES), f32),
+            shape((n_shard, 16, LANES), bf16),
+        ],
+        in_specs=[vmem] * 13,
+        out_specs=[vmem] * 5,
+        scratch_shapes=[
+            pltpu.VMEM((2 * key_rows, width), bf16),
+            pltpu.VMEM((2 * router_rows, width), bf16),
+            pltpu.VMEM((2 * rank, LANES), f32),
+            pltpu.VMEM((n_dp, 8, LANES), f32),
+            pltpu.VMEM((total, 8, LANES), f32),
+            pltpu.VMEM((1, 16, LANES), bf16),
+            pltpu.VMEM((n_dp, 16, LANES), bf16),
+            pltpu.VMEM((total,) + chunk, bf16),
+            pltpu.VMEM((half,) + chunk, bf16),
+            pltpu.VMEM((half,) + chunk, bf16),
+            pltpu.VMEM((half,) + chunk, bf16),
+            pltpu.SemaphoreType.DMA((9,)),
+            pltpu.SemaphoreType.DMA((9,)),
+        ],
+        compiler_params=pltpu.CompilerParams(
+            collective_id=0, has_side_effects=True, vmem_limit_bytes=32 * 2**20
+        ),
+        name="exchange",
+    )(
+        key_grad, key_error, router_grad, router_error, norm_grad, key_basis, router_basis,
+        key_momentum, key_weight, router_momentum, router_weight, norm_momentum, norm_weight,
+    )
+    return pl.pallas_call(
+        functools.partial(finish_kernel, n_dp, n_shard, rank),
+        out_shape=[
+            shape(key_error.shape, f32),
+            shape(router_error.shape, f32),
+            shape(key_momentum.shape, f32),
+            shape(key_momentum.shape, f32),
+            shape((n_shard * key_rows, span), bf16),
+            shape(router_momentum.shape, f32),
+            shape(router_momentum.shape, f32),
+            shape((n_shard * router_rows, span), bf16),
+            shape(norm_momentum.shape, f32),
+            shape(norm_momentum.shape, f32),
+            shape((norm_momentum.shape[0], width), bf16),
+        ],
+        in_specs=[vmem] * 15,
+        out_specs=[vmem] * 11,
+        scratch_shapes=[
+            pltpu.VMEM((2 * rank, width), bf16),
+            pltpu.VMEM((2 * rank, width), bf16),
+        ],
+        compiler_params=pltpu.CompilerParams(vmem_limit_bytes=32 * 2**20),
+        name="finish",
+    )(
+        key_grad, key_error, router_grad, router_error, key_momentum, key_weight,
+        router_momentum, router_weight, norm_momentum, norm_weight, *middle,
+    )
+
+
 def solution(mesh):
+    n_dp, n_shard = mesh.shape["dp"], mesh.shape["shard"]
+
+    def body(*arrays):
+        key_grad, router_grad, key_basis = arrays[0], arrays[2], arrays[5]
+        rank, width = key_basis.shape
+        tiled = (
+            2 * rank == 8 * n_dp == 16 * n_shard
+            and key_grad.shape[1] == LANES
+            and router_grad.shape[1] == 16
+            and 2 * width == 5 * LANES * n_dp
+            and arrays[11].shape == (2, 5 * LANES)
+        )
+        if tiled:
+            return fast_body(n_dp, n_shard, *arrays)
+        return general_body(*arrays)
+
     return jax.shard_map(
         body,
         mesh=mesh,

time: 224 us -> 50.7 us (0.23)
  waiting for transfers between devices: 120 us -> 0 us
  blocking collectives: 66.1 us -> 0 us
  Pallas kernels: 0 us -> 35.2 us
  between operations: 15.8 us -> 0.68 us
  matrix products: 11.1 us -> 0 us
  local copies, waits for them, and re-layouts: 4.05 us -> 14.2 us
  other arithmetic: 6.77 us -> 0 us
    psum x1 -> x0, waiting for transfers between devices: 120 us -> none  [body(): lax.psum(jnp.concatenate([key_part, router_part], axis=1), ('dp', 'shard'))]
    psum x2 -> x0, blocking collectives: 49.1 us -> none  [the longest x1 38.9 us: body(): lax.psum((project(key_basis, merged_key), project(router_basis, merged_ro...]
    pallas_call x0 -> x2, Pallas kernels: none -> 35.2 us  [the longest x1 33.4 us: fast_body(): pl.pallas_call(functools.partial(exchange_kernel, n_dp, n_shard, rank), o...]
    all_gather x3 -> x0, blocking collectives: 16.9 us -> none  [the longest x1 6.55 us: body(): lax.all_gather(key_master.astype(jnp.bfloat16), 'shard', axis=0, tiled=True)]
    dot_general x32 -> x0, matrix products: 11.1 us -> none  [the longest x2 4.36 us: project(): lax.dot_general(old_basis, merged, (((1,), (1,)), ((), ())), precision=hi...]
    unnamed x29 -> x24, local copies, waits for them, and re-layouts: 4.05 us -> 11.8 us
    pallas_call x0 -> x3, local copies, waits for them, and re-layouts: none -> 2.46 us  [fast_body(): pl.pallas_call(functools.partial(finish_kernel, n_dp, n_shard, rank), out...]
  transfers between devices with their start and end apart: 1 -> 0, of which waited for: 1 -> 0; matrix products, arithmetic and copies ran while one was open for 0% -> 0% of each run, Pallas kernels for 0% -> 0%
where the time goes in v1:
time: 50.7 us; the launch traced here: 50.1 us
  Pallas kernels  35.2 us (69%)
  local copies, waits for them, and re-layouts  14.2 us (28%)
  between operations  0.68 us (1%)
    pallas_call x1, Pallas kernels, fast_body(): pl.pallas_call(functools.partial(exchange_kernel, n_dp, n_shard, rank), o...  33.4 us
    unnamed x24, local copies, waits for them, and re-layouts  11.8 us
    pallas_call x3, local copies, waits for them, and re-layouts, fast_body(): pl.pallas_call(functools.partial(finish_kernel, n_dp, n_shard, rank), out...  2.46 us
    pallas_call x1, Pallas kernels, fast_body(): pl.pallas_call(functools.partial(finish_kernel, n_dp, n_shard, rank), out...  1.87 us

profile of v1, /device:TPU:0, one launch (start us, length us, event | category | flops | bytes accessed | tf_op | source)
XLA Modules:
  0.0 50.1 jit_solution(5378015129547868425)
XLA Ops:
  0.6 1.0 %copy.26.km = f32[128,320]{1,0:T(8,128)S(1)} copy(f32[128,320]{0,1:T(8,128)} %param.20) | data formatting | bytes 327680 | tf_op args[7]
  1.7 1.0 %copy.27.kw = f32[128,320]{1,0:T(8,128)S(1)} copy(f32[128,320]{0,1:T(8,128)} %param.21) | data formatting | bytes 327680 | tf_op args[8]
  2.7 0.0 copy-start
  2.7 1.3 %copy-done = f32[1,128,2560]{2,1,0:T(8,128)S(1)} copy-done((f32[1,128,2560]{2,1,0:T(8,128)S(1)}, f32[1,128,2560]{2,1,0:T(8,128)}, u32[]{:S(2)}) %copy-start) | copy-done | bytes 1310744
  4.1 0.0 copy-start.1
  4.1 1.1 %copy-done.1 = bf16[1,128,2560]{2,1,0:T(8,128)(2,1)S(1)} copy-done((bf16[1,128,2560]{2,1,0:T(8,128)(2,1)S(1)}, bf16[1,128,2560]{2,1,0:T(8,128)(2,1)}, u32[]{:S(2)}) %copy-start.1) | copy-done | bytes 655384
  5.1 0.0 copy-start.2
  5.1 0.9 %copy-done.2 = f32[1,16,2560]{2,1,0:T(8,128)S(1)} copy-done((f32[1,16,2560]{2,1,0:T(8,128)S(1)}, f32[1,16,2560]{2,1,0:T(8,128)}, u32[]{:S(2)}) %copy-start.2) | copy-done | bytes 163864
  6.1 0.0 copy-start.3
  6.1 1.0 %copy-done.3 = f32[32,2560]{1,0:T(8,128)S(1)} copy-done((f32[32,2560]{1,0:T(8,128)S(1)}, f32[32,2560]{1,0:T(8,128)}, u32[]{:S(2)}) %copy-start.3) | copy-done | bytes 327704
  7.0 0.0 copy-start.4
  7.0 1.0 %copy-done.4 = f32[32,2560]{1,0:T(8,128)S(1)} copy-done((f32[32,2560]{1,0:T(8,128)S(1)}, f32[32,2560]{1,0:T(8,128)}, u32[]{:S(2)}) %copy-start.4) | copy-done | bytes 327704
  8.0 0.0 copy-start.5
  8.0 0.9 %copy-done.5 = bf16[1,16,2560]{2,1,0:T(8,128)(2,1)S(1)} copy-done((bf16[1,16,2560]{2,1,0:T(8,128)(2,1)S(1)}, bf16[1,16,2560]{2,1,0:T(8,128)(2,1)}, u32[]{:S(2)}) %copy-start.5) | copy-done | bytes 81944
  8.9 0.0 copy-start.6
  8.9 0.7 %copy-done.6 = f32[16,320]{1,0:T(8,128)S(1)} copy-done((f32[16,320]{1,0:T(8,128)S(1)}, f32[16,320]{1,0:T(8,128)}, u32[]{:S(2)}) %copy-start.6) | copy-done | bytes 20504
  9.6 0.0 copy-start.7
  9.6 0.7 %copy-done.7 = f32[16,320]{1,0:T(8,128)S(1)} copy-done((f32[16,320]{1,0:T(8,128)S(1)}, f32[16,320]{1,0:T(8,128)}, u32[]{:S(2)}) %copy-start.7) | copy-done | bytes 20504
  10.4 0.0 copy-start.8
  10.4 0.7 %copy-done.8 = f32[2,640]{1,0:T(2,128)S(1)} copy-done((f32[2,640]{1,0:T(2,128)S(1)}, f32[2,640]{1,0:T(2,128)}, u32[]{:S(2)}) %copy-start.8) | copy-done | bytes 5144
  11.1 0.0 copy-start.9
  11.1 0.7 %copy-done.9 = f32[2,640]{1,0:T(2,128)S(1)} copy-done((f32[2,640]{1,0:T(2,128)S(1)}, f32[2,640]{1,0:T(2,128)}, u32[]{:S(2)}) %copy-start.9) | copy-done | bytes 5144
  11.8 0.0 copy-start.10
  11.8 0.7 %copy-done.10 = bf16[1,2,640]{2,1,0:T(2,128)(2,1)S(1)} copy-done((bf16[1,2,640]{2,1,0:T(2,128)(2,1)S(1)}, bf16[1,2,640]{2,1,0:T(2,128)(2,1)}, u32[]{:S(2)}) %copy-start.10) | copy-done | bytes 2584
  12.4 33.4 %exchange.1 = (f32[64,512]{1,0:T(8,128)S(1)}, bf16[32,16,384]{2,1,0:T(8,128)(2,1)S(1)}, bf16[4,144,320]{2,1,0:T(8,128)(2,1)S(1)}, f32[16,128]{1,0:T(8,128)S(1)}, bf16[4,16,128]{2,1,0:T(8,128)(2,1)S(1)}) custom-call(bf16[1,128,2560]{2,1,0:T(8,128)(2,1)S(1)} %copy-done.1, f32[1,128,2560]{2,1,0:T(8,128)S(1)} %copy-done, bf16[1,16,2560]{2,1,0:T(8,128)(2,1)S(1)} %copy-done.5, ...), custom_call_target="tpu_custom_call" | custom-call | tf_op jit(solution)/shard_map/exchange/pallas_call | solution.py:424
  45.8 1.9 %finish.1 = (f32[1,128,2560]{2,1,0:T(8,128)}, f32[1,16,2560]{2,1,0:T(8,128)}, f32[128,320]{1,0:T(8,128)S(1)}, f32[128,320]{1,0:T(8,128)S(1)}, bf16[512,320]{1,0:...) custom-call(bf16[1,128,2560]{2,1,0:T(8,128)(2,1)S(1)} %copy-done.1, ...), custom_call_target="tpu_custom_call" | custom-call | tf_op jit(solution)/shard_map/finish/pallas_call | solution.py:458
  47.7 0.8 %copy.28 = f32[128,320]{0,1:T(8,128)} copy(f32[128,320]{1,0:T(8,128)S(1)} %get-tuple-element.23) | data formatting | bytes 327680 | tf_op jit(solution)/shard_map/finish/pallas_call | solution.py:458
  48.5 0.8 %copy.29 = f32[128,320]{0,1:T(8,128)} copy(f32[128,320]{1,0:T(8,128)S(1)} %get-tuple-element.24) | data formatting | bytes 327680 | tf_op jit(solution)/shard_map/finish/pallas_call | solution.py:458
  49.2 0.9 %copy.30 = bf16[512,320]{0,1:T(8,128)(2,1)} copy(bf16[512,320]{1,0:T(8,128)(2,1)S(1)} %get-tuple-element.25) | data formatting | bytes 655360 | tf_op jit(solution)/shard_map/finish/pallas_call | solution.py:458
Async XLA Ops:
  2.7 1.3 %copy-start = (f32[1,128,2560]{2,1,0:T(8,128)S(1)}, f32[1,128,2560]{2,1,0:T(8,128)}, u32[]{:S(2)}) copy-start(f32[1,128,2560]{2,1,0:T(8,128)} %ke.3) | copy-start | bytes 3932164
  4.1 1.1 %copy-start.1 = (bf16[1,128,2560]{2,1,0:T(8,128)(2,1)S(1)}, bf16[1,128,2560]{2,1,0:T(8,128)(2,1)}, u32[]{:S(2)}) copy-start(bf16[1,128,2560]{2,1,0:T(8,128)(2,1)} %kg.3) | copy-start | bytes 1966084
  5.1 0.9 %copy-start.2 = (f32[1,16,2560]{2,1,0:T(8,128)S(1)}, f32[1,16,2560]{2,1,0:T(8,128)}, u32[]{:S(2)}) copy-start(f32[1,16,2560]{2,1,0:T(8,128)} %re.3) | copy-start | bytes 491524
  6.1 1.0 %copy-start.3 = (f32[32,2560]{1,0:T(8,128)S(1)}, f32[32,2560]{1,0:T(8,128)}, u32[]{:S(2)}) copy-start(f32[32,2560]{1,0:T(8,128)} %kb.1) | copy-start | bytes 983044
  7.0 1.0 %copy-start.4 = (f32[32,2560]{1,0:T(8,128)S(1)}, f32[32,2560]{1,0:T(8,128)}, u32[]{:S(2)}) copy-start(f32[32,2560]{1,0:T(8,128)} %rb.1) | copy-start | bytes 983044
  8.0 0.9 %copy-start.5 = (bf16[1,16,2560]{2,1,0:T(8,128)(2,1)S(1)}, bf16[1,16,2560]{2,1,0:T(8,128)(2,1)}, u32[]{:S(2)}) copy-start(bf16[1,16,2560]{2,1,0:T(8,128)(2,1)} %rg.3) | copy-start | bytes 245764
  8.9 0.7 %copy-start.6 = (f32[16,320]{1,0:T(8,128)S(1)}, f32[16,320]{1,0:T(8,128)}, u32[]{:S(2)}) copy-start(f32[16,320]{1,0:T(8,128)} %rm.3) | copy-start | bytes 61444
  9.6 0.7 %copy-start.7 = (f32[16,320]{1,0:T(8,128)S(1)}, f32[16,320]{1,0:T(8,128)}, u32[]{:S(2)}) copy-start(f32[16,320]{1,0:T(8,128)} %rw.3) | copy-start | bytes 61444
  10.4 0.7 %copy-start.8 = (f32[2,640]{1,0:T(2,128)S(1)}, f32[2,640]{1,0:T(2,128)}, u32[]{:S(2)}) copy-start(f32[2,640]{1,0:T(2,128)} %nm.3) | copy-start | bytes 15364
  11.1 0.7 %copy-start.9 = (f32[2,640]{1,0:T(2,128)S(1)}, f32[2,640]{1,0:T(2,128)}, u32[]{:S(2)}) copy-start(f32[2,640]{1,0:T(2,128)} %nw.3) | copy-start | bytes 15364
  11.8 0.7 %copy-start.10 = (bf16[1,2,640]{2,1,0:T(2,128)(2,1)S(1)}, bf16[1,2,640]{2,1,0:T(2,128)(2,1)}, u32[]{:S(2)}) copy-start(bf16[1,2,640]{2,1,0:T(2,128)(2,1)} %ng.1) | copy-start | bytes 7684

commit v2 on v1

--- a/solution.py
+++ b/solution.py
@@ -133,8 +133,8 @@
     return y[:, :cols] + y[:, cols:]
 
 
-def window(d):
-    return (5 * d // 2) * LANES
+def tile_start(d):
+    return (5 * d + 1) // 2
 
 
 def packed(x):
@@ -143,11 +143,31 @@
     return jnp.concatenate(pieces + [jnp.zeros((16 - rows, LANES), f32)], axis=0)
 
 
+NT = (((1,), (1,)), ((), ()))
+
+
+def dot(a, b):
+    return jnp.dot(a, b, preferred_element_type=f32)
+
+
+def dot_nt(a, b):
+    return lax.dot_general(a, b, NT, preferred_element_type=f32)
+
+
+def mul(a, b, product=dot):
+    a_high, a_low = halves(a)
+    b_high, b_low = halves(b)
+    both = product(jnp.concatenate([a_high, a_low], axis=0), b_high)
+    rows = a.shape[0]
+    return both[:rows] + (both[rows:] + product(a_high, b_low))
+
+
 def exchange_kernel(
     n_dp, n_shard, rank,
-    kg, ke, rg, re, ng, kb, rb, km, kw, rm, rw, nm, nw,
-    ortho, cols, ufull, nsum, npar,
-    mk, mr, p64, recv1, recv2, nsend, nrecv, csend, crecv, bsend, brecv, send, recv,
+    kg_h, ke_h, rg_h, re_h, kb_h, rb_h, ng_h, nm_h, nw_h, km_h, kw_h, rm_h, rw_h,
+    mk, mr, km, kw, rm, rw, nm, nw, ortho, cols, ukey, urouter, nsum, npar,
+    kg, ke, rg, re, kb, rb, ng,
+    mkm, mrm, p64, recv1, recv2, nsend, nrecv, csend, brecv, load, send, recv,
 ):
     d = lax.axis_index("dp")
     s = lax.axis_index("shard")
@@ -158,8 +178,23 @@
     mate = s + 1 - 2 * core
     half = total // 2
     q = x * n_dp + d
-    key_rows, width = mk.shape[0] // 2, mk.shape[1]
+    key_rows = mk.shape[0] // 2
     router_rows = mr.shape[0] // 2
+    tiles = csend.shape[0] // 2
+
+    fetched = {}
+    pairs = dict(
+        kg=(kg_h, kg), ke=(ke_h, ke), kb=(kb_h, kb), rg=(rg_h, rg), re=(re_h, re), rb=(rb_h, rb),
+        ng=(ng_h, ng), nm=(nm_h, nm), nw=(nw_h, nw), km=(km_h, km), kw=(kw_h, kw),
+        rm=(rm_h, rm), rw=(rw_h, rw),
+    )
+    for index, (name, (there, here)) in enumerate(pairs.items()):
+        fetched[name] = pltpu.make_async_copy(there, here, load.at[index])
+        fetched[name].start()
+
+    def need(*names):
+        for name in names:
+            fetched[name].wait()
 
     def peer_all(j):
         t = lax.rem(me + j, total)
@@ -185,21 +220,26 @@
     def wait_send(ref, which):
         pltpu.make_async_copy(ref, ref, send.at[which]).wait()
 
+    need("kg", "ke")
     high, low = halves(kg[0].astype(f32) + ke[0])
     mk[:key_rows] = high
     mk[key_rows:] = low
+    need("kb")
+    kb2 = jnp.concatenate(halves(kb[...]), axis=0)
+    p64[:rank] = fold(dot_nt(kb2, mk[...]), rank, key_rows)
+    need("rg", "re", "rb")
     high, low = halves(rg[0].astype(f32) + re[0])
     mr[:router_rows] = high
     mr[router_rows:] = low
-    nt = (((1,), (1,)), ((), ()))
-    kb2 = jnp.concatenate(halves(kb[...]), axis=0)
-    pk = lax.dot_general(kb2, mk[...], nt, preferred_element_type=f32)
-    p64[:rank] = fold(pk, rank, key_rows)
     rb2 = jnp.concatenate(halves(rb[...]), axis=0)
-    pr = lax.dot_general(rb2, mr[...], nt, preferred_element_type=f32)
     p64[rank:] = jnp.concatenate(
-        [fold(pr, rank, router_rows), jnp.zeros((rank, LANES - router_rows), f32)], axis=1
-    )
+        [
+            fold(dot_nt(rb2, mr[...]), rank, router_rows),
+            jnp.zeros((rank, LANES - router_rows), f32),
+        ],
+        axis=1,
+    )
+    need("ng")
     nsend[0] = packed(ng[0].astype(f32)).astype(bf16)
 
     pl.semaphore_wait(barrier, total - 1)
@@ -217,6 +257,15 @@
         return carry
 
     lax.fori_loop(1, n_dp, send_norm, 0)
+
+    @pl.when(core == 1)
+    def _():
+        put(mk, mkm, 5, (d, mate))
+
+    @pl.when(core == 0)
+    def _():
+        put(mr, mrm, 5, (d, mate))
+
     recv1[d] = p64[pl.ds(pl.multiple_of(d * 8, 8), 8), :]
     nrecv[d] = nsend[0]
     wait_recv(recv1.at[pl.ds(0, n_dp - 1)], 0)
@@ -230,11 +279,15 @@
     lax.fori_loop(1, total, send_sum, 0)
 
     decay = learning_rate * momentum_decay
-    ufull[s, :key_rows] = (kw[...] - decay * km[...]).astype(bf16)
-    ufull[s, key_rows:] = (rw[...] - decay * rm[...]).astype(bf16)
+    need("km", "kw", "rm", "rw")
+    ukey[s] = (kw[...] - decay * km[...]).astype(bf16)
+    urouter[s] = (rw[...] - decay * rm[...]).astype(bf16)
     for j in range(1, n_shard):
-        put(ufull.at[s], ufull.at[s], 3, (d, lax.rem(s + j, n_shard)))
-
+        to = (d, lax.rem(s + j, n_shard))
+        put(ukey.at[s], ukey.at[s], 3, to)
+        put(urouter.at[s], urouter.at[s], 9, to)
+
+    need("nm", "nw")
     wait_recv(nrecv.at[pl.ds(0, n_dp - 1)], 1)
     norm_sum = jnp.sum(nrecv[...].astype(f32), axis=0)
     nsum[...] = norm_sum
@@ -251,18 +304,13 @@
     )
     down = lax.broadcasted_iota(jnp.int32, (both, both), 0)
     along = lax.broadcasted_iota(jnp.int32, (both, both), 1)
-    gram = lax.dot_general(rows, rows, nt, precision=highest, preferred_element_type=f32)
-    gram = jnp.where((down < rank) == (along < rank), gram, 0.0)
+    gram = jnp.where((down < rank) == (along < rank), mul(rows, rows, dot_nt), 0.0)
     identity = jnp.where(down == along, 1.0, 0.0).astype(f32)
     square = gram * gram
     scale_key = jnp.sqrt(jnp.sum(square[:rank], keepdims=True)) + 1e-06
     scale_router = jnp.sqrt(jnp.sum(square[rank:], keepdims=True)) + 1e-06
     row_index = lax.broadcasted_iota(jnp.int32, (both, 1), 0)
     scaling = jnp.where(row_index < rank, scale_key, scale_router)
-
-    def mul(a, b):
-        return jnp.dot(a, b, precision=highest, preferred_element_type=f32)
-
     t = gram / scaling
     middle = 1.5 * identity - 0.5 * t
     root = middle
@@ -273,129 +321,166 @@
             root = mul(middle, root)
     ortho[...] = mul(middle, mul(root, rows)) / jnp.sqrt(scaling)
 
-    own = ortho[:, pl.ds(pl.multiple_of(s * LANES, LANES), LANES)]
+    def factor(which):
+        return ortho[:, pl.ds(pl.multiple_of(which * LANES, LANES), LANES)]
 
     def columns_of(factor, merged):
         high, low = halves(factor)
         left = jnp.concatenate(
             [jnp.concatenate([high, high], axis=1), jnp.concatenate([low, low], axis=1)], axis=0
         )
-        out = jnp.dot(left, merged, preferred_element_type=f32)
+        out = dot(left, merged)
         return out[:rank] + out[rank:]
 
-    part_key = columns_of(own[:rank], mk[...]).astype(bf16)
-    part_router = columns_of(own[rank:, :router_rows], mr[...]).astype(bf16)
-    for k in range(n_shard):
-        part = part_key if k < n_shard // 2 else part_router
-        top = 16 * (k % (n_shard // 2))
-        for b in range(n_dp):
-            at = (k % 2) * half + (k // 2) * n_dp + b
-            csend[at] = part[top : top + 16, window(b) : window(b) + 3 * LANES]
-
-    there = csend.at[pl.ds((1 - core) * half, half)]
-    put(there, crecv, 5, (d, mate))
-    wait_recv(crecv, 5)
-    bsend[...] = (csend[pl.ds(core * half, half)].astype(f32) + crecv[...].astype(f32)).astype(bf16)
+    def keep(part):
+        part = part.astype(bf16)
+        for k in range(2):
+            for j in range(tiles):
+                csend[k * tiles + j] = part[16 * k : 16 * k + 16, LANES * j : LANES * (j + 1)]
+
+    @pl.when(core == 0)
+    def _():
+        wait_recv(mkm, 5)
+        keep(columns_of(factor(s)[:rank], mk[...]) + columns_of(factor(mate)[:rank], mkm[...]))
+
+    @pl.when(core == 1)
+    def _():
+        wait_recv(mrm, 5)
+        keep(
+            columns_of(factor(s)[rank:, :router_rows], mr[...])
+            + columns_of(factor(mate)[rank:, :router_rows], mrm[...])
+        )
 
     def peer_core(j):
         to = lax.rem(q + j, half)
-        return to, (lax.rem(to, n_dp), (to // n_dp) * 2 + core)
+        return to // n_dp, lax.rem(to, n_dp)
 
     def send_part(j, carry):
-        to, device = peer_core(j)
-        put(bsend.at[to], brecv.at[q], 6, device)
+        to_x, to_d = peer_core(j)
+        first = to_x * tiles + tile_start(to_d)
+        for parity, count in ((0, 3), (1, 2)):
+
+            @pl.when(lax.rem(to_d, 2) == parity)
+            def _():
+                put(
+                    csend.at[pl.ds(first, count)], brecv.at[q, pl.ds(0, count)], 6,
+                    (to_d, to_x * 2 + core),
+                )
+
         return carry
 
     lax.fori_loop(1, half, send_part, 0)
-    brecv[q] = bsend[q]
-    wait_recv(brecv.at[pl.ds(0, half - 1)], 6)
-    mine = core * half + q
-    cols[mine] = (jnp.sum(brecv[...].astype(f32), axis=0) / n_dp).astype(bf16)
-
-    def send_columns(j, carry):
-        to, device = peer_core(j)
-        put(cols.at[mine], cols.at[mine], 7, device)
-        return carry
-
-    lax.fori_loop(1, half, send_columns, 0)
-    wait_recv(cols.at[pl.ds(0, half - 1)], 7)
-    ours = cols.at[pl.ds(core * half, half)]
+    offset = x * tiles + tile_start(d)
+    mine = core * 2 * tiles + offset
+    for parity, count in ((0, 3), (1, 2)):
+
+        @pl.when(lax.rem(d, 2) == parity)
+        def _():
+            brecv[q, :count] = csend[pl.ds(offset, count)]
+            wait_recv(cols.at[pl.ds(0, (half - 1) * count)], 6)
+            added = jnp.sum(brecv[:, :count].astype(f32), axis=0) / n_dp
+            cols[pl.ds(mine, count)] = added.astype(bf16)
+
+            def send_columns(j, carry):
+                to_x, to_d = peer_core(j)
+                there = cols.at[pl.ds(mine, count)]
+                put(there, there, 7, (to_d, to_x * 2 + core))
+                return carry
+
+            lax.fori_loop(1, half, send_columns, 0)
+            wait_recv(cols.at[pl.ds(0, 2 * tiles - count)], 7)
+
+    ours = cols.at[pl.ds(core * 2 * tiles, 2 * tiles)]
     put(ours, ours, 8, (d, mate))
 
-    wait_recv(ufull.at[pl.ds(0, n_shard - 1)], 3)
+    wait_recv(ukey.at[pl.ds(0, n_shard - 1)], 3)
+    wait_recv(urouter.at[pl.ds(0, n_shard - 1)], 9)
     wait_recv(npar.at[pl.ds(0, n_shard - 1)], 4)
     wait_send(recv1.at[pl.ds(0, n_dp - 1)], 0)
     wait_send(nrecv.at[pl.ds(0, n_dp - 1)], 1)
     wait_send(recv2.at[pl.ds(0, total - 1)], 2)
-    wait_send(ufull.at[pl.ds(0, n_shard - 1)], 3)
+    wait_send(ukey.at[pl.ds(0, n_shard - 1)], 3)
+    wait_send(urouter.at[pl.ds(0, n_shard - 1)], 9)
     wait_send(npar.at[pl.ds(0, n_shard - 1)], 4)
-    wait_send(crecv, 5)
-    wait_send(brecv.at[pl.ds(0, half - 1)], 6)
-    wait_send(cols.at[pl.ds(0, half - 1)], 7)
+
+    @pl.when(core == 1)
+    def _():
+        wait_send(mk, 5)
+
+    @pl.when(core == 0)
+    def _():
+        wait_send(mr, 5)
+
+    for parity, count in ((0, 3), (1, 2)):
+
+        @pl.when(lax.rem(d, 2) == parity)
+        def _():
+            wait_send(csend.at[pl.ds(0, 2 * tiles - count)], 6)
+            wait_send(cols.at[pl.ds(0, (half - 1) * count)], 7)
+
     wait_recv(ours, 8)
     wait_send(ours, 8)
 
 
 def finish_kernel(
     n_dp, n_shard, rank,
-    kg, ke, rg, re, km, kw, rm, rw, nm, nw, ortho, cols, ufull, nsum, npar,
+    mk, mr, km, kw, rm, rw, nm, nw, ortho, cols, ukey, urouter, nsum, npar,
     key_carry, router_carry, key_velocity, key_master, key_params,
     router_velocity, router_master, router_params, norm_velocity, norm_master, norm_params,
     ck, cr,
 ):
     d = lax.axis_index("dp")
     s = lax.axis_index("shard")
-    half = n_dp * n_shard // 2
-    key_rows, router_rows = kg.shape[1], rg.shape[1]
-    span = km.shape[1]
-    for k in range(n_shard):
-        where = ck if k < n_shard // 2 else cr
-        top = 16 * (k % (n_shard // 2))
-        for b in range(n_dp):
-            at = (k % 2) * half + (k // 2) * n_dp + b
-            skip = LANES if b % 2 else 0
-            piece = cols[at][:, skip:]
-            lane = window(b) + skip
-            where[top : top + 16, lane : window(b) + 3 * LANES] = piece
-            where[rank + top : rank + top + 16, lane : window(b) + 3 * LANES] = piece
+    key_rows, router_rows = mk.shape[0] // 2, mr.shape[0] // 2
+    span = km.shape[0]
+    tiles = cols.shape[0] // 4
+    for core, where in ((0, ck), (1, cr)):
+        for k in range(2):
+            for j in range(tiles):
+                piece = cols[(core * 2 + k) * tiles + j]
+                lanes = slice(LANES * j, LANES * (j + 1))
+                where[16 * k : 16 * k + 16, lanes] = piece
+                where[rank + 16 * k : rank + 16 * k + 16, lanes] = piece
 
     def turned(factor):
         return jnp.concatenate(halves(factor.T), axis=1)
-
-    def dot(a, b):
-        return jnp.dot(a, b, preferred_element_type=f32)
 
     own = ortho[:, pl.ds(pl.multiple_of(s * LANES, LANES), LANES)]
     own_key = turned(own[:rank])
     own_router = turned(own[rank:])[:router_rows]
-    key_carry[0] = kg[0].astype(f32) + ke[0] - dot(own_key, ck[...])
-    router_carry[0] = rg[0].astype(f32) + re[0] - dot(own_router, cr[...])
-
-    def block(first):
+    merged = mk[:key_rows].astype(f32) + mk[key_rows:].astype(f32)
+    key_carry[0] = merged - dot(own_key, ck[...])
+    merged = mr[:router_rows].astype(f32) + mr[router_rows:].astype(f32)
+    router_carry[0] = merged - dot(own_router, cr[...])
+
+    def block(core):
         parts = []
-        for k in (first, first + 1):
-            parts.append(cols[(k % 2) * half + (k // 2) * n_dp + d].astype(f32))
+        for k in range(2):
+            near = cols[pl.ds((core * 2 + k) * tiles + 5 * d // 2, 3)].astype(f32)
+            parts.append(jnp.concatenate([near[0], near[1], near[2]], axis=1))
         both = jnp.concatenate(parts, axis=0)
         extra = both.shape[1] - span
-        picked = jnp.where(lax.rem(d, 2) == 1, both[:, extra:], both[:, :span]).astype(bf16)
-        return jnp.concatenate([picked, picked], axis=0)
-
-    block_key = block(0)
-    block_router = block(n_shard // 2)
-    key_velocity[...], key_master[...] = advance(km[...], kw[...], dot(own_key, block_key))
+        return jnp.where(lax.rem(d, 2) == 1, both[:, extra:], both[:, :span])
+
+    turned_block = block(0).T.astype(bf16)
+    key_block = jnp.concatenate([turned_block, turned_block], axis=1)
+    router_block = block(1).astype(bf16)
+    router_block = jnp.concatenate([router_block, router_block], axis=0)
+    key_velocity[...], key_master[...] = advance(
+        km[...], kw[...], dot(key_block, jnp.concatenate(halves(own[:rank]), axis=0))
+    )
     router_velocity[...], router_master[...] = advance(
-        rm[...], rw[...], dot(own_router, block_router)
-    )
+        rm[...], rw[...], dot(own_router, router_block)
+    )
+    approx = dot(key_block, jnp.concatenate(halves(ortho[:rank]), axis=0))
     for k in range(n_shard):
-        factor = ortho[:, LANES * k : LANES * (k + 1)]
-        approx = dot(turned(factor[:rank]), block_key)
-        held = ufull[k].astype(f32)
-        key_params[key_rows * k : key_rows * (k + 1)] = (
-            held[:key_rows] - learning_rate * approx
+        lanes = slice(key_rows * k, key_rows * (k + 1))
+        key_params[:, lanes] = (
+            ukey[k].astype(f32) - learning_rate * approx[:, lanes]
         ).astype(bf16)
-        approx = dot(turned(factor[rank:])[:router_rows], block_router)
+        factor = turned(ortho[rank:, LANES * k : LANES * (k + 1)])[:router_rows]
         router_params[router_rows * k : router_rows * (k + 1)] = (
-            held[key_rows:] - learning_rate * approx
+            urouter[k].astype(f32) - learning_rate * dot(factor, router_block)
         ).astype(bf16)
 
     pieces = nm.shape[1] // LANES
@@ -417,22 +502,40 @@
     rank, width = key_basis.shape
     key_rows, router_rows = key_grad.shape[1], router_grad.shape[1]
     span = key_momentum.shape[1]
-    total, half = n_dp * n_shard, n_dp * n_shard // 2
+    total, half, tiles = n_dp * n_shard, n_dp * n_shard // 2, width // LANES
     vmem = pl.BlockSpec(memory_space=pltpu.VMEM)
+    hbm = pl.BlockSpec(memory_space=pltpu.HBM)
     shape = jax.ShapeDtypeStruct
-    chunk = (16, 3 * LANES)
+    key_state, router_state = shape((span, key_rows), f32), shape((router_rows, span), f32)
+    norm_state = shape(norm_momentum.shape, f32)
     middle = pl.pallas_call(
         functools.partial(exchange_kernel, n_dp, n_shard, rank),
         out_shape=[
+            shape((2 * key_rows, width), bf16),
+            shape((2 * router_rows, width), bf16),
+            key_state,
+            key_state,
+            router_state,
+            router_state,
+            norm_state,
+            norm_state,
             shape((2 * rank, n_shard * LANES), f32),
-            shape((total,) + chunk, bf16),
-            shape((n_shard, key_rows + router_rows, span), bf16),
+            shape((4 * tiles, 16, LANES), bf16),
+            shape((n_shard, span, key_rows), bf16),
+            shape((n_shard, router_rows, span), bf16),
             shape((16, LANES), f32),
             shape((n_shard, 16, LANES), bf16),
         ],
-        in_specs=[vmem] * 13,
-        out_specs=[vmem] * 5,
+        in_specs=[hbm] * 13,
+        out_specs=[vmem] * 14,
         scratch_shapes=[
+            pltpu.VMEM(key_grad.shape, bf16),
+            pltpu.VMEM(key_error.shape, f32),
+            pltpu.VMEM(router_grad.shape, bf16),
+            pltpu.VMEM(router_error.shape, f32),
+            pltpu.VMEM(key_basis.shape, f32),
+            pltpu.VMEM(router_basis.shape, f32),
+            pltpu.VMEM(norm_grad.shape, bf16),
             pltpu.VMEM((2 * key_rows, width), bf16),
             pltpu.VMEM((2 * router_rows, width), bf16),
             pltpu.VMEM((2 * rank, LANES), f32),
@@ -440,48 +543,51 @@
             pltpu.VMEM((total, 8, LANES), f32),
             pltpu.VMEM((1, 16, LANES), bf16),
             pltpu.VMEM((n_dp, 16, LANES), bf16),
-            pltpu.VMEM((total,) + chunk, bf16),
-            pltpu.VMEM((half,) + chunk, bf16),
-            pltpu.VMEM((half,) + chunk, bf16),
-            pltpu.VMEM((half,) + chunk, bf16),
-            pltpu.SemaphoreType.DMA((9,)),
-            pltpu.SemaphoreType.DMA((9,)),
+            pltpu.VMEM((2 * tiles, 16, LANES), bf16),
+            pltpu.VMEM((half, 3, 16, LANES), bf16),
+            pltpu.SemaphoreType.DMA((13,)),
+            pltpu.SemaphoreType.DMA((10,)),
+            pltpu.SemaphoreType.DMA((10,)),
         ],
         compiler_params=pltpu.CompilerParams(
-            collective_id=0, has_side_effects=True, vmem_limit_bytes=32 * 2**20
+            collective_id=0, has_side_effects=True, vmem_limit_bytes=24 * 2**20
         ),
         name="exchange",
     )(
-        key_grad, key_error, router_grad, router_error, norm_grad, key_basis, router_basis,
-        key_momentum, key_weight, router_momentum, router_weight, norm_momentum, norm_weight,
-    )
-    return pl.pallas_call(
+        *(
+            pltpu.with_memory_space_constraint(operand, pltpu.HBM)
+            for operand in (
+                key_grad, key_error, router_grad, router_error, key_basis, router_basis, norm_grad,
+                norm_momentum, norm_weight, key_momentum.T, key_weight.T, router_momentum,
+                router_weight,
+            )
+        )
+    )
+    results = pl.pallas_call(
         functools.partial(finish_kernel, n_dp, n_shard, rank),
         out_shape=[
             shape(key_error.shape, f32),
             shape(router_error.shape, f32),
-            shape(key_momentum.shape, f32),
-            shape(key_momentum.shape, f32),
-            shape((n_shard * key_rows, span), bf16),
-            shape(router_momentum.shape, f32),
-            shape(router_momentum.shape, f32),
+            key_state,
+            key_state,
+            shape((span, n_shard * key_rows), bf16),
+            router_state,
+            router_state,
             shape((n_shard * router_rows, span), bf16),
-            shape(norm_momentum.shape, f32),
-            shape(norm_momentum.shape, f32),
+            norm_state,
+            norm_state,
             shape((norm_momentum.shape[0], width), bf16),
         ],
-        in_specs=[vmem] * 15,
+        in_specs=[vmem] * 14,
         out_specs=[vmem] * 11,
         scratch_shapes=[
             pltpu.VMEM((2 * rank, width), bf16),
             pltpu.VMEM((2 * rank, width), bf16),
         ],
-        compiler_params=pltpu.CompilerParams(vmem_limit_bytes=32 * 2**20),
+        compiler_params=pltpu.CompilerParams(vmem_limit_bytes=24 * 2**20),
         name="finish",
-    )(
-        key_grad, key_error, router_grad, router_error, key_momentum, key_weight,
-        router_momentum, router_weight, norm_momentum, norm_weight, *middle,
-    )
+    )(*middle)
+    return tuple(y.T if i in (2, 3, 4) else y for i, y in enumerate(results))
 
 
 def solution(mesh):

time: 50.7 us -> 33.2 us (0.65)
  local copies, waits for them, and re-layouts: 14.2 us -> 0 us
  Pallas kernels: 35.2 us -> 32.4 us
    unnamed x24 -> x0, local copies, waits for them, and re-layouts: 11.8 us -> none
    pallas_call x1, Pallas kernels: 33.4 us -> 30.3 us  [fast_body(): pl.pallas_call(functools.partial(exchange_kernel, n_dp, n_shard, rank), o...]
    pallas_call x3 -> x0, local copies, waits for them, and re-layouts: 2.46 us -> none  [fast_body(): pl.pallas_call(functools.partial(finish_kernel, n_dp, n_shard, rank), out...]
where the time goes in v2:
time: 33.2 us; the launch traced here: 33 us
  Pallas kernels  32.4 us (98%)
  between operations  0.66 us (2%)
    pallas_call x1, Pallas kernels, fast_body(): pl.pallas_call(functools.partial(exchange_kernel, n_dp, n_shard, rank), o...  30.3 us
    pallas_call x1, Pallas kernels, fast_body(): pl.pallas_call(functools.partial(finish_kernel, n_dp, n_shard, rank), out...  2.12 us

profile of v2, /device:TPU:0, one launch (start us, length us, event | category | flops | bytes accessed | tf_op | source)
XLA Modules:
  0.0 33.0 jit_solution(2481545226231589756)
XLA Ops:
  0.6 30.3 %exchange.1 = (bf16[256,2560]{1,0:T(8,128)(2,1)S(1)}, bf16[32,2560]{1,0:T(8,128)(2,1)S(1)}, f32[320,128]{1,0:T(8,128)S(1)}, f32[320,128]{1,0:T(8,128)S(1)}, f32[...) custom-call(bf16[1,128,2560]{2,1,0:T(8,128)(2,1)} %kg_h.1, ...), custom_call_target="tpu_custom_call" | custom-call | tf_op jit(solution)/shard_map/exchange/pallas_call | solution.py:511
  30.9 2.1 %finish.1 = (f32[1,128,2560]{2,1,0:T(8,128)}, f32[1,16,2560]{2,1,0:T(8,128)}, f32[320,128]{1,0:T(8,128)}, f32[320,128]{1,0:T(8,128)}, bf16[320,512]{1,0:T(8,128)...) custom-call(bf16[256,2560]{1,0:T(8,128)(2,1)S(1)} %get-tuple-element, ...), custom_call_target="tpu_custom_call" | custom-call | tf_op jit(solution)/shard_map/finish/pallas_call | solution.py:566

commit v3 on v2

--- a/solution.py
+++ b/solution.py
@@ -182,19 +182,33 @@
     router_rows = mr.shape[0] // 2
     tiles = csend.shape[0] // 2
 
+    pairs = n_dp // 2
+    span = mk.shape[1] // pairs
+    chunks = [slice(span * p, span * (p + 1)) for p in range(pairs)]
     fetched = {}
-    pairs = dict(
-        kg=(kg_h, kg), ke=(ke_h, ke), kb=(kb_h, kb), rg=(rg_h, rg), re=(re_h, re), rb=(rb_h, rb),
-        ng=(ng_h, ng), nm=(nm_h, nm), nw=(nw_h, nw), km=(km_h, km), kw=(kw_h, kw),
-        rm=(rm_h, rm), rw=(rw_h, rw),
-    )
-    for index, (name, (there, here)) in enumerate(pairs.items()):
-        fetched[name] = pltpu.make_async_copy(there, here, load.at[index])
+
+    def fetch(name, there, here):
+        fetched[name] = pltpu.make_async_copy(there, here, load.at[len(fetched)])
         fetched[name].start()
 
     def need(*names):
         for name in names:
             fetched[name].wait()
+
+    fetch("rg", rg_h, rg)
+    fetch("re", re_h, re)
+    fetch("rb", rb_h, rb)
+    for p, lanes in enumerate(chunks):
+        fetch(("kg", p), kg_h.at[:, :, lanes], kg.at[:, :, lanes])
+        fetch(("ke", p), ke_h.at[:, :, lanes], ke.at[:, :, lanes])
+        fetch(("kb", p), kb_h.at[:, lanes], kb.at[:, lanes])
+    fetch("ng", ng_h, ng)
+    fetch("km", km_h, km)
+    fetch("kw", kw_h, kw)
+    fetch("rm", rm_h, rm)
+    fetch("rw", rw_h, rw)
+    fetch("nm", nm_h, nm)
+    fetch("nw", nw_h, nw)
 
     def peer_all(j):
         t = lax.rem(me + j, total)
@@ -220,13 +234,6 @@
     def wait_send(ref, which):
         pltpu.make_async_copy(ref, ref, send.at[which]).wait()
 
-    need("kg", "ke")
-    high, low = halves(kg[0].astype(f32) + ke[0])
-    mk[:key_rows] = high
-    mk[key_rows:] = low
-    need("kb")
-    kb2 = jnp.concatenate(halves(kb[...]), axis=0)
-    p64[:rank] = fold(dot_nt(kb2, mk[...]), rank, key_rows)
     need("rg", "re", "rb")
     high, low = halves(rg[0].astype(f32) + re[0])
     mr[:router_rows] = high
@@ -239,24 +246,38 @@
         ],
         axis=1,
     )
+    projected = None
+    for p, lanes in enumerate(chunks):
+        need(("kg", p), ("ke", p), ("kb", p))
+        high, low = halves(kg[0, :, lanes].astype(f32) + ke[0, :, lanes])
+        mk[:key_rows, lanes] = high
+        mk[key_rows:, lanes] = low
+        kb2 = jnp.concatenate(halves(kb[:, lanes]), axis=0)
+        term = dot_nt(kb2, jnp.concatenate([high, low], axis=0))
+        projected = term if projected is None else projected + term
+    p64[:rank] = fold(projected, rank, key_rows)
+
+    pl.semaphore_wait(barrier, total - 1)
+
+    def far_first(count):
+        return sorted(range(1, count), key=lambda j: -min(j, count - j))
+
+    for j in far_first(n_dp):
+        to = lax.rem(d + j, n_dp)
+        put(p64.at[pl.ds(pl.multiple_of(to * 8, 8), 8)], recv1.at[d], 0, (to, s))
+    recv1[d] = p64[pl.ds(pl.multiple_of(d * 8, 8), 8), :]
     need("ng")
     nsend[0] = packed(ng[0].astype(f32)).astype(bf16)
-
-    pl.semaphore_wait(barrier, total - 1)
-
-    def send_rows(j, carry):
-        t = lax.rem(d + j, n_dp)
-        put(p64.at[pl.ds(pl.multiple_of(t * 8, 8), 8)], recv1.at[d], 0, (t, s))
-        return carry
-
-    lax.fori_loop(1, n_dp, send_rows, 0)
-
-    def send_norm(j, carry):
-        t = lax.rem(d + j, n_dp)
-        put(nsend.at[0], nrecv.at[d], 1, (t, s))
-        return carry
-
-    lax.fori_loop(1, n_dp, send_norm, 0)
+    nrecv[d] = nsend[0]
+    need("km", "kw", "rm", "rw")
+    decay = learning_rate * momentum_decay
+    ukey[s] = (kw[...] - decay * km[...]).astype(bf16)
+    urouter[s] = (rw[...] - decay * rm[...]).astype(bf16)
+    wait_recv(recv1.at[pl.ds(0, n_dp - 1)], 0)
+    slot = s * n_dp + d
+    recv2[slot] = jnp.sum(recv1[...], axis=0)
+    for j in far_first(total):
+        put(recv2.at[slot], recv2.at[slot], 2, peer_all(j))
 
     @pl.when(core == 1)
     def _():
@@ -266,37 +287,15 @@
     def _():
         put(mr, mrm, 5, (d, mate))
 
-    recv1[d] = p64[pl.ds(pl.multiple_of(d * 8, 8), 8), :]
-    nrecv[d] = nsend[0]
-    wait_recv(recv1.at[pl.ds(0, n_dp - 1)], 0)
-    slot = s * n_dp + d
-    recv2[slot] = jnp.sum(recv1[...], axis=0)
-
-    def send_sum(j, carry):
-        put(recv2.at[slot], recv2.at[slot], 2, peer_all(j))
-        return carry
-
-    lax.fori_loop(1, total, send_sum, 0)
-
-    decay = learning_rate * momentum_decay
-    need("km", "kw", "rm", "rw")
-    ukey[s] = (kw[...] - decay * km[...]).astype(bf16)
-    urouter[s] = (rw[...] - decay * rm[...]).astype(bf16)
+    for j in range(1, n_dp):
+        put(nsend.at[0], nrecv.at[d], 1, (lax.rem(d + j, n_dp), s))
+
+    wait_recv(recv2.at[pl.ds(0, total - 1)], 2)
+
     for j in range(1, n_shard):
         to = (d, lax.rem(s + j, n_shard))
         put(ukey.at[s], ukey.at[s], 3, to)
         put(urouter.at[s], urouter.at[s], 9, to)
-
-    need("nm", "nw")
-    wait_recv(nrecv.at[pl.ds(0, n_dp - 1)], 1)
-    norm_sum = jnp.sum(nrecv[...].astype(f32), axis=0)
-    nsum[...] = norm_sum
-    norm_velocity, norm_master = advance(packed(nm[...]), packed(nw[...]), norm_sum / n_dp)
-    npar[s] = norm_master.astype(bf16)
-    for j in range(1, n_shard):
-        put(npar.at[s], npar.at[s], 4, (d, lax.rem(s + j, n_shard)))
-
-    wait_recv(recv2.at[pl.ds(0, total - 1)], 2)
 
     both = 2 * rank
     rows = jnp.concatenate(
@@ -324,52 +323,66 @@
     def factor(which):
         return ortho[:, pl.ds(pl.multiple_of(which * LANES, LANES), LANES)]
 
-    def columns_of(factor, merged):
+    def stacked(factor):
         high, low = halves(factor)
-        left = jnp.concatenate(
+        return jnp.concatenate(
             [jnp.concatenate([high, high], axis=1), jnp.concatenate([low, low], axis=1)], axis=0
         )
-        out = dot(left, merged)
-        return out[:rank] + out[rank:]
-
-    def keep(part):
-        part = part.astype(bf16)
-        for k in range(2):
-            for j in range(tiles):
-                csend[k * tiles + j] = part[16 * k : 16 * k + 16, LANES * j : LANES * (j + 1)]
+
+    per_pair = tiles // pairs
+
+    def columns_of(owner, left_own, own_ref, left_mate, mate_ref):
+        for step in (2, 1, 3, 0):
+            p = lax.rem(d // 2 + step, pairs)
+            lanes = pl.ds(pl.multiple_of(p * span, LANES), span)
+            out = dot(left_own, own_ref[:, lanes]) + dot(left_mate, mate_ref[:, lanes])
+            part = (out[:rank] + out[rank:]).astype(bf16)
+            for k in range(2):
+                for j in range(per_pair):
+                    csend[k * tiles + per_pair * p + j] = part[
+                        16 * k : 16 * k + 16, LANES * j : LANES * (j + 1)
+                    ]
+            for k in range(2):
+                for odd, first, count in ((0, 0, 3), (1, 3, 2)):
+                    to_d = 2 * p + odd
+
+                    def send_part():
+                        put(
+                            csend.at[pl.ds(k * tiles + per_pair * p + first, count)],
+                            brecv.at[q, pl.ds(0, count)], 6, (to_d, 2 * k + owner),
+                        )
+
+                    if step:
+                        send_part()
+                    else:
+                        pl.when(jnp.logical_or(x != k, to_d != d))(send_part)
 
     @pl.when(core == 0)
     def _():
+        own, other = stacked(factor(s)[:rank]), stacked(factor(mate)[:rank])
         wait_recv(mkm, 5)
-        keep(columns_of(factor(s)[:rank], mk[...]) + columns_of(factor(mate)[:rank], mkm[...]))
+        columns_of(0, own, mk, other, mkm)
 
     @pl.when(core == 1)
     def _():
+        own = stacked(factor(s)[rank:, :router_rows])
+        other = stacked(factor(mate)[rank:, :router_rows])
         wait_recv(mrm, 5)
-        keep(
-            columns_of(factor(s)[rank:, :router_rows], mr[...])
-            + columns_of(factor(mate)[rank:, :router_rows], mrm[...])
-        )
+        columns_of(1, own, mr, other, mrm)
+
+    need("nm", "nw")
+    wait_recv(nrecv.at[pl.ds(0, n_dp - 1)], 1)
+    norm_sum = jnp.sum(nrecv[...].astype(f32), axis=0)
+    nsum[...] = norm_sum
+    norm_velocity, norm_master = advance(packed(nm[...]), packed(nw[...]), norm_sum / n_dp)
+    npar[s] = norm_master.astype(bf16)
+    for j in range(1, n_shard):
+        put(npar.at[s], npar.at[s], 4, (d, lax.rem(s + j, n_shard)))
 
     def peer_core(j):
         to = lax.rem(q + j, half)
         return to // n_dp, lax.rem(to, n_dp)
 
-    def send_part(j, carry):
-        to_x, to_d = peer_core(j)
-        first = to_x * tiles + tile_start(to_d)
-        for parity, count in ((0, 3), (1, 2)):
-
-            @pl.when(lax.rem(to_d, 2) == parity)
-            def _():
-                put(
-                    csend.at[pl.ds(first, count)], brecv.at[q, pl.ds(0, count)], 6,
-                    (to_d, to_x * 2 + core),
-                )
-
-        return carry
-
-    lax.fori_loop(1, half, send_part, 0)
     offset = x * tiles + tile_start(d)
     mine = core * 2 * tiles + offset
     for parity, count in ((0, 3), (1, 2)):
@@ -381,17 +394,17 @@
             added = jnp.sum(brecv[:, :count].astype(f32), axis=0) / n_dp
             cols[pl.ds(mine, count)] = added.astype(bf16)
 
-            def send_columns(j, carry):
+            there = cols.at[pl.ds(mine, count)]
+            for j in far_first(half):
                 to_x, to_d = peer_core(j)
-                there = cols.at[pl.ds(mine, count)]
-                put(there, there, 7, (to_d, to_x * 2 + core))
-                return carry
-
-            lax.fori_loop(1, half, send_columns, 0)
-            wait_recv(cols.at[pl.ds(0, 2 * tiles - count)], 7)
-
-    ours = cols.at[pl.ds(core * 2 * tiles, 2 * tiles)]
+                put(there, there, 7 + 3 * lax.rem(to_x + x, 2), (to_d, to_x * 2 + core))
+            wait_recv(cols.at[pl.ds(0, tiles - count)], 7)
+
+    ours = cols.at[pl.ds(core * 2 * tiles + x * tiles, tiles)]
     put(ours, ours, 8, (d, mate))
+    theirs = cols.at[pl.ds(core * 2 * tiles + (1 - x) * tiles, tiles)]
+    wait_recv(theirs, 10)
+    put(theirs, theirs, 11, (d, mate))
 
     wait_recv(ukey.at[pl.ds(0, n_shard - 1)], 3)
     wait_recv(urouter.at[pl.ds(0, n_shard - 1)], 9)
@@ -416,10 +429,13 @@
         @pl.when(lax.rem(d, 2) == parity)
         def _():
             wait_send(csend.at[pl.ds(0, 2 * tiles - count)], 6)
-            wait_send(cols.at[pl.ds(0, (half - 1) * count)], 7)
-
+            wait_send(cols.at[pl.ds(0, (n_dp - 1) * count)], 7)
+            wait_send(cols.at[pl.ds(0, n_dp * count)], 10)
+
+    wait_send(ours, 8)
+    wait_send(theirs, 11)
     wait_recv(ours, 8)
-    wait_send(ours, 8)
+    wait_recv(theirs, 11)
 
 
 def finish_kernel(
@@ -427,20 +443,24 @@
     mk, mr, km, kw, rm, rw, nm, nw, ortho, cols, ukey, urouter, nsum, npar,
     key_carry, router_carry, key_velocity, key_master, key_params,
     router_velocity, router_master, router_params, norm_velocity, norm_master, norm_params,
-    ck, cr,
+    carry, out,
 ):
     d = lax.axis_index("dp")
     s = lax.axis_index("shard")
     key_rows, router_rows = mk.shape[0] // 2, mr.shape[0] // 2
     span = km.shape[0]
     tiles = cols.shape[0] // 4
-    for core, where in ((0, ck), (1, cr)):
-        for k in range(2):
-            for j in range(tiles):
-                piece = cols[(core * 2 + k) * tiles + j]
-                lanes = slice(LANES * j, LANES * (j + 1))
-                where[16 * k : 16 * k + 16, lanes] = piece
-                where[rank + 16 * k : rank + 16 * k + 16, lanes] = piece
+    pairs = n_dp // 2
+    per_pair = tiles // pairs
+
+    def columns(core, p):
+        parts = [
+            jnp.concatenate(
+                [cols[(core * 2 + k) * tiles + per_pair * p + j] for j in range(per_pair)], axis=1
+            )
+            for k in range(2)
+        ]
+        return jnp.concatenate(parts + parts, axis=0)
 
     def turned(factor):
         return jnp.concatenate(halves(factor.T), axis=1)
@@ -448,10 +468,19 @@
     own = ortho[:, pl.ds(pl.multiple_of(s * LANES, LANES), LANES)]
     own_key = turned(own[:rank])
     own_router = turned(own[rank:])[:router_rows]
-    merged = mk[:key_rows].astype(f32) + mk[key_rows:].astype(f32)
-    key_carry[0] = merged - dot(own_key, ck[...])
-    merged = mr[:router_rows].astype(f32) + mr[router_rows:].astype(f32)
-    router_carry[0] = merged - dot(own_router, cr[...])
+    copies = []
+    for p in range(pairs):
+        lanes = slice(LANES * per_pair * p, LANES * per_pair * (p + 1))
+        merged = mk[:key_rows, lanes].astype(f32) + mk[key_rows:, lanes].astype(f32)
+        carry[0, :, lanes] = merged - dot(own_key, columns(0, p))
+        copies.append(
+            pltpu.make_async_copy(
+                carry.at[:, :, lanes], key_carry.at[:, :, lanes], out.at[p]
+            )
+        )
+        copies[-1].start()
+        merged = mr[:router_rows, lanes].astype(f32) + mr[router_rows:, lanes].astype(f32)
+        router_carry[0, :, lanes] = merged - dot(own_router, columns(1, p))
 
     def block(core):
         parts = []
@@ -492,6 +521,8 @@
     norm_params[...] = jnp.concatenate(
         [unpacked(npar[k].astype(f32)) for k in range(n_shard)], axis=1
     ).astype(bf16)
+    for copy in copies:
+        copy.wait()
 
 
 def fast_body(
@@ -545,9 +576,9 @@
             pltpu.VMEM((n_dp, 16, LANES), bf16),
             pltpu.VMEM((2 * tiles, 16, LANES), bf16),
             pltpu.VMEM((half, 3, 16, LANES), bf16),
-            pltpu.SemaphoreType.DMA((13,)),
-            pltpu.SemaphoreType.DMA((10,)),
-            pltpu.SemaphoreType.DMA((10,)),
+            pltpu.SemaphoreType.DMA((10 + 3 * n_dp // 2,)),
+            pltpu.SemaphoreType.DMA((12,)),
+            pltpu.SemaphoreType.DMA((12,)),
         ],
         compiler_params=pltpu.CompilerParams(
             collective_id=0, has_side_effects=True, vmem_limit_bytes=24 * 2**20
@@ -579,10 +610,10 @@
             shape((norm_momentum.shape[0], width), bf16),
         ],
         in_specs=[vmem] * 14,
-        out_specs=[vmem] * 11,
+        out_specs=[hbm] + [vmem] * 10,
         scratch_shapes=[
-            pltpu.VMEM((2 * rank, width), bf16),
-            pltpu.VMEM((2 * rank, width), bf16),
+            pltpu.VMEM(key_error.shape, f32),
+            pltpu.SemaphoreType.DMA((n_dp // 2,)),
         ],
         compiler_params=pltpu.CompilerParams(vmem_limit_bytes=24 * 2**20),
         name="finish",

time: 33.2 us -> 34.5 us (1.039)
  Pallas kernels: 32.4 us -> 33.7 us
    pallas_call x1, Pallas kernels: 30.3 us -> 31.3 us  [fast_body(): pl.pallas_call(functools.partial(exchange_kernel, n_dp, n_shard, rank), o...]
where the time goes in v3:
time: 34.5 us; the launch traced here: 34.4 us
  Pallas kernels  33.7 us (98%)
  between operations  0.66 us (2%)
    pallas_call x1, Pallas kernels, fast_body(): pl.pallas_call(functools.partial(exchange_kernel, n_dp, n_shard, rank), o...  31.3 us
    pallas_call x1, Pallas kernels, fast_body(): pl.pallas_call(functools.partial(finish_kernel, n_dp, n_shard, rank), out...  2.44 us

profile of v3, /device:TPU:0, one launch (start us, length us, event | category | flops | bytes accessed | tf_op | source)
XLA Modules:
  0.0 34.4 jit_solution(14425984026472782769)
XLA Ops:
  0.6 31.3 %exchange.1 = (bf16[256,2560]{1,0:T(8,128)(2,1)S(1)}, bf16[32,2560]{1,0:T(8,128)(2,1)S(1)}, f32[320,128]{1,0:T(8,128)S(1)}, f32[320,128]{1,0:T(8,128)S(1)}, f32[...) custom-call(bf16[1,128,2560]{2,1,0:T(8,128)(2,1)} %kg_h.1, ...), custom_call_target="tpu_custom_call" | custom-call | tf_op jit(solution)/shard_map/exchange/pallas_call | solution.py:542
  31.9 2.4 %finish.1 = (f32[1,128,2560]{2,1,0:T(8,128)}, f32[1,16,2560]{2,1,0:T(8,128)}, f32[320,128]{1,0:T(8,128)}, f32[320,128]{1,0:T(8,128)}, bf16[320,512]{1,0:T(8,128)...) custom-call(bf16[256,2560]{1,0:T(8,128)(2,1)S(1)} %get-tuple-element, ...), custom_call_target="tpu_custom_call" | custom-call | tf_op jit(solution)/shard_map/finish/pallas_call | solution.py:597

commit v4 on v3

--- a/solution.py
+++ b/solution.py
@@ -165,7 +165,7 @@
 def exchange_kernel(
     n_dp, n_shard, rank,
     kg_h, ke_h, rg_h, re_h, kb_h, rb_h, ng_h, nm_h, nw_h, km_h, kw_h, rm_h, rw_h,
-    mk, mr, km, kw, rm, rw, nm, nw, ortho, cols, ukey, urouter, nsum, npar,
+    mk, mr, km, kw, rm, rw, nm, nw, lift, cols, ukey, urouter, nsum, npar,
     kg, ke, rg, re, kb, rb, ng,
     mkm, mrm, p64, recv1, recv2, nsend, nrecv, csend, brecv, load, send, recv,
 ):
@@ -238,6 +238,7 @@
     high, low = halves(rg[0].astype(f32) + re[0])
     mr[:router_rows] = high
     mr[router_rows:] = low
+    mrm[:router_rows] = high
     rb2 = jnp.concatenate(halves(rb[...]), axis=0)
     p64[rank:] = jnp.concatenate(
         [
@@ -252,6 +253,7 @@
         high, low = halves(kg[0, :, lanes].astype(f32) + ke[0, :, lanes])
         mk[:key_rows, lanes] = high
         mk[key_rows:, lanes] = low
+        mkm[:key_rows, lanes] = high
         kb2 = jnp.concatenate(halves(kb[:, lanes]), axis=0)
         term = dot_nt(kb2, jnp.concatenate([high, low], axis=0))
         projected = term if projected is None else projected + term
@@ -265,6 +267,17 @@
     for j in far_first(n_dp):
         to = lax.rem(d + j, n_dp)
         put(p64.at[pl.ds(pl.multiple_of(to * 8, 8), 8)], recv1.at[d], 0, (to, s))
+
+    key_half, router_half = pl.ds(key_rows, key_rows), pl.ds(router_rows, router_rows)
+
+    @pl.when(core == 1)
+    def _():
+        put(mk.at[pl.ds(0, key_rows)], mkm.at[key_half], 5, (d, mate))
+
+    @pl.when(core == 0)
+    def _():
+        put(mr.at[pl.ds(0, router_rows)], mrm.at[router_half], 5, (d, mate))
+
     recv1[d] = p64[pl.ds(pl.multiple_of(d * 8, 8), 8), :]
     need("ng")
     nsend[0] = packed(ng[0].astype(f32)).astype(bf16)
@@ -276,26 +289,73 @@
     wait_recv(recv1.at[pl.ds(0, n_dp - 1)], 0)
     slot = s * n_dp + d
     recv2[slot] = jnp.sum(recv1[...], axis=0)
-    for j in far_first(total):
-        put(recv2.at[slot], recv2.at[slot], 2, peer_all(j))
-
-    @pl.when(core == 1)
-    def _():
-        put(mk, mkm, 5, (d, mate))
-
-    @pl.when(core == 0)
-    def _():
-        put(mr, mrm, 5, (d, mate))
+    summed = recv2.at[slot]
+    for j in far_first(n_dp):
+        put(summed, summed, 2, (lax.rem(d + j, n_dp), s))
+    for j in far_first(n_dp) + [0]:
+        put(summed, summed, 2, (lax.rem(d + j, n_dp), mate))
+    for j in far_first(n_dp) + [0]:
+        for other in range(2):
+            put(summed, summed, 12, (lax.rem(d + j, n_dp), 2 * (1 - x) + other))
 
     for j in range(1, n_dp):
         put(nsend.at[0], nrecv.at[d], 1, (lax.rem(d + j, n_dp), s))
-
-    wait_recv(recv2.at[pl.ds(0, total - 1)], 2)
 
     for j in range(1, n_shard):
         to = (d, lax.rem(s + j, n_shard))
         put(ukey.at[s], ukey.at[s], 3, to)
         put(urouter.at[s], urouter.at[s], 9, to)
+
+    wait_recv(recv2.at[pl.ds(0, half - 1)], 2)
+
+    def factor(which, first):
+        count = rank // 8
+        return recv2[pl.ds(which * n_dp + first * count, count)].reshape(rank, LANES)
+
+    def stacked(own, other):
+        return jnp.concatenate(halves(jnp.concatenate([own, other], axis=1)), axis=0)
+
+    per_pair = tiles // pairs
+
+    def columns_of(owner, left, merged):
+        for step in (2, 1, 3, 0):
+            p = lax.rem(d // 2 + step, pairs)
+            lanes = pl.ds(pl.multiple_of(p * span, LANES), span)
+            out = dot(left, merged[:, lanes])
+            part = (out[:rank] + out[rank:]).astype(bf16)
+            for k in range(2):
+                for j in range(per_pair):
+                    csend[k * tiles + per_pair * p + j] = part[
+                        16 * k : 16 * k + 16, LANES * j : LANES * (j + 1)
+                    ]
+            for k in range(2):
+                for odd, first, count in ((0, 0, 3), (1, 3, 2)):
+                    to_d = 2 * p + odd
+
+                    def send_part():
+                        put(
+                            csend.at[pl.ds(k * tiles + per_pair * p + first, count)],
+                            brecv.at[q, pl.ds(0, count)], 6, (to_d, 2 * k + owner),
+                        )
+
+                    if step:
+                        send_part()
+                    else:
+                        pl.when(jnp.logical_or(x != k, to_d != d))(send_part)
+
+    @pl.when(core == 0)
+    def _():
+        left = stacked(factor(s, 0), factor(mate, 0))
+        wait_recv(mkm.at[key_half], 5)
+        columns_of(0, left, mkm)
+
+    @pl.when(core == 1)
+    def _():
+        left = stacked(factor(s, 1)[:, :router_rows], factor(mate, 1)[:, :router_rows])
+        wait_recv(mrm.at[router_half], 5)
+        columns_of(1, left, mrm)
+
+    wait_recv(recv2.at[pl.ds(0, half)], 12)
 
     both = 2 * rank
     rows = jnp.concatenate(
@@ -318,57 +378,8 @@
         middle = 1.5 * identity - 0.5 * t
         if step < ROOT_STEPS - 1:
             root = mul(middle, root)
-    ortho[...] = mul(middle, mul(root, rows)) / jnp.sqrt(scaling)
-
-    def factor(which):
-        return ortho[:, pl.ds(pl.multiple_of(which * LANES, LANES), LANES)]
-
-    def stacked(factor):
-        high, low = halves(factor)
-        return jnp.concatenate(
-            [jnp.concatenate([high, high], axis=1), jnp.concatenate([low, low], axis=1)], axis=0
-        )
-
-    per_pair = tiles // pairs
-
-    def columns_of(owner, left_own, own_ref, left_mate, mate_ref):
-        for step in (2, 1, 3, 0):
-            p = lax.rem(d // 2 + step, pairs)
-            lanes = pl.ds(pl.multiple_of(p * span, LANES), span)
-            out = dot(left_own, own_ref[:, lanes]) + dot(left_mate, mate_ref[:, lanes])
-            part = (out[:rank] + out[rank:]).astype(bf16)
-            for k in range(2):
-                for j in range(per_pair):
-                    csend[k * tiles + per_pair * p + j] = part[
-                        16 * k : 16 * k + 16, LANES * j : LANES * (j + 1)
-                    ]
-            for k in range(2):
-                for odd, first, count in ((0, 0, 3), (1, 3, 2)):
-                    to_d = 2 * p + odd
-
-                    def send_part():
-                        put(
-                            csend.at[pl.ds(k * tiles + per_pair * p + first, count)],
-                            brecv.at[q, pl.ds(0, count)], 6, (to_d, 2 * k + owner),
-                        )
-
-                    if step:
-                        send_part()
-                    else:
-                        pl.when(jnp.logical_or(x != k, to_d != d))(send_part)
-
-    @pl.when(core == 0)
-    def _():
-        own, other = stacked(factor(s)[:rank]), stacked(factor(mate)[:rank])
-        wait_recv(mkm, 5)
-        columns_of(0, own, mk, other, mkm)
-
-    @pl.when(core == 1)
-    def _():
-        own = stacked(factor(s)[rank:, :router_rows])
-        other = stacked(factor(mate)[rank:, :router_rows])
-        wait_recv(mrm, 5)
-        columns_of(1, own, mr, other, mrm)
+    root = mul(middle, root)
+    lift[...] = mul(root, mul(root, rows)) / scaling
 
     need("nm", "nw")
     wait_recv(nrecv.at[pl.ds(0, n_dp - 1)], 1)
@@ -411,18 +422,19 @@
     wait_recv(npar.at[pl.ds(0, n_shard - 1)], 4)
     wait_send(recv1.at[pl.ds(0, n_dp - 1)], 0)
     wait_send(nrecv.at[pl.ds(0, n_dp - 1)], 1)
-    wait_send(recv2.at[pl.ds(0, total - 1)], 2)
+    wait_send(recv2.at[pl.ds(0, half - 1)], 2)
+    wait_send(recv2.at[pl.ds(0, half)], 12)
     wait_send(ukey.at[pl.ds(0, n_shard - 1)], 3)
     wait_send(urouter.at[pl.ds(0, n_shard - 1)], 9)
     wait_send(npar.at[pl.ds(0, n_shard - 1)], 4)
 
     @pl.when(core == 1)
     def _():
-        wait_send(mk, 5)
+        wait_send(mkm.at[key_half], 5)
 
     @pl.when(core == 0)
     def _():
-        wait_send(mr, 5)
+        wait_send(mrm.at[router_half], 5)
 
     for parity, count in ((0, 3), (1, 2)):
 
@@ -440,47 +452,34 @@
 
 def finish_kernel(
     n_dp, n_shard, rank,
-    mk, mr, km, kw, rm, rw, nm, nw, ortho, cols, ukey, urouter, nsum, npar,
+    mk, mr, km, kw, rm, rw, nm, nw, lift, cols, ukey, urouter, nsum, npar,
     key_carry, router_carry, key_velocity, key_master, key_params,
     router_velocity, router_master, router_params, norm_velocity, norm_master, norm_params,
-    carry, out,
+    ck, cr,
 ):
     d = lax.axis_index("dp")
     s = lax.axis_index("shard")
     key_rows, router_rows = mk.shape[0] // 2, mr.shape[0] // 2
     span = km.shape[0]
     tiles = cols.shape[0] // 4
-    pairs = n_dp // 2
-    per_pair = tiles // pairs
-
-    def columns(core, p):
-        parts = [
-            jnp.concatenate(
-                [cols[(core * 2 + k) * tiles + per_pair * p + j] for j in range(per_pair)], axis=1
-            )
-            for k in range(2)
-        ]
-        return jnp.concatenate(parts + parts, axis=0)
+    for core, where in ((0, ck), (1, cr)):
+        for k in range(2):
+            for j in range(tiles):
+                piece = cols[(core * 2 + k) * tiles + j]
+                lanes = slice(LANES * j, LANES * (j + 1))
+                where[16 * k : 16 * k + 16, lanes] = piece
+                where[rank + 16 * k : rank + 16 * k + 16, lanes] = piece
 
     def turned(factor):
         return jnp.concatenate(halves(factor.T), axis=1)
 
-    own = ortho[:, pl.ds(pl.multiple_of(s * LANES, LANES), LANES)]
+    own = lift[:, pl.ds(pl.multiple_of(s * LANES, LANES), LANES)]
     own_key = turned(own[:rank])
     own_router = turned(own[rank:])[:router_rows]
-    copies = []
-    for p in range(pairs):
-        lanes = slice(LANES * per_pair * p, LANES * per_pair * (p + 1))
-        merged = mk[:key_rows, lanes].astype(f32) + mk[key_rows:, lanes].astype(f32)
-        carry[0, :, lanes] = merged - dot(own_key, columns(0, p))
-        copies.append(
-            pltpu.make_async_copy(
-                carry.at[:, :, lanes], key_carry.at[:, :, lanes], out.at[p]
-            )
-        )
-        copies[-1].start()
-        merged = mr[:router_rows, lanes].astype(f32) + mr[router_rows:, lanes].astype(f32)
-        router_carry[0, :, lanes] = merged - dot(own_router, columns(1, p))
+    merged = mk[:key_rows].astype(f32) + mk[key_rows:].astype(f32)
+    key_carry[0] = merged - dot(own_key, ck[...])
+    merged = mr[:router_rows].astype(f32) + mr[router_rows:].astype(f32)
+    router_carry[0] = merged - dot(own_router, cr[...])
 
     def block(core):
         parts = []
@@ -501,13 +500,13 @@
     router_velocity[...], router_master[...] = advance(
         rm[...], rw[...], dot(own_router, router_block)
     )
-    approx = dot(key_block, jnp.concatenate(halves(ortho[:rank]), axis=0))
+    approx = dot(key_block, jnp.concatenate(halves(lift[:rank]), axis=0))
     for k in range(n_shard):
         lanes = slice(key_rows * k, key_rows * (k + 1))
         key_params[:, lanes] = (
             ukey[k].astype(f32) - learning_rate * approx[:, lanes]
         ).astype(bf16)
-        factor = turned(ortho[rank:, LANES * k : LANES * (k + 1)])[:router_rows]
+        factor = turned(lift[rank:, LANES * k : LANES * (k + 1)])[:router_rows]
         router_params[router_rows * k : router_rows * (k + 1)] = (
             urouter[k].astype(f32) - learning_rate * dot(factor, router_block)
         ).astype(bf16)
@@ -521,8 +520,6 @@
     norm_params[...] = jnp.concatenate(
         [unpacked(npar[k].astype(f32)) for k in range(n_shard)], axis=1
     ).astype(bf16)
-    for copy in copies:
-        copy.wait()
 
 
 def fast_body(
@@ -577,8 +574,8 @@
             pltpu.VMEM((2 * tiles, 16, LANES), bf16),
             pltpu.VMEM((half, 3, 16, LANES), bf16),
             pltpu.SemaphoreType.DMA((10 + 3 * n_dp // 2,)),
-            pltpu.SemaphoreType.DMA((12,)),
-            pltpu.SemaphoreType.DMA((12,)),
+            pltpu.SemaphoreType.DMA((13,)),
+            pltpu.SemaphoreType.DMA((13,)),
         ],
         compiler_params=pltpu.CompilerParams(
             collective_id=0, has_side_effects=True, vmem_limit_bytes=24 * 2**20
@@ -610,10 +607,10 @@
             shape((norm_momentum.shape[0], width), bf16),
         ],
         in_specs=[vmem] * 14,
-        out_specs=[hbm] + [vmem] * 10,
+        out_specs=[vmem] * 11,
         scratch_shapes=[
-            pltpu.VMEM(key_error.shape, f32),
-            pltpu.SemaphoreType.DMA((n_dp // 2,)),
+            pltpu.VMEM((2 * rank, width), bf16),
+            pltpu.VMEM((2 * rank, width), bf16),
         ],
         compiler_params=pltpu.CompilerParams(vmem_limit_bytes=24 * 2**20),
         name="finish",

time: 34.5 us -> 31.7 us (0.919)
  Pallas kernels: 33.7 us -> 30.9 us
    pallas_call x1, Pallas kernels: 31.3 us -> 28.8 us  [fast_body(): pl.pallas_call(functools.partial(exchange_kernel, n_dp, n_shard, rank), o...]
where the time goes in v4:
time: 31.7 us; the launch traced here: 31.6 us
  Pallas kernels  30.9 us (97%)
  between operations  0.66 us (2%)
    pallas_call x1, Pallas kernels, fast_body(): pl.pallas_call(functools.partial(exchange_kernel, n_dp, n_shard, rank), o...  28.8 us
    pallas_call x1, Pallas kernels, fast_body(): pl.pallas_call(functools.partial(finish_kernel, n_dp, n_shard, rank), out...  2.12 us

profile of v4, /device:TPU:0, one launch (start us, length us, event | category | flops | bytes accessed | tf_op | source)
XLA Modules:
  0.0 31.6 jit_solution(2763893915182143910)
XLA Ops:
  0.6 28.8 %exchange.1 = (bf16[256,2560]{1,0:T(8,128)(2,1)S(1)}, bf16[32,2560]{1,0:T(8,128)(2,1)S(1)}, f32[320,128]{1,0:T(8,128)S(1)}, f32[320,128]{1,0:T(8,128)S(1)}, f32[...) custom-call(bf16[1,128,2560]{2,1,0:T(8,128)(2,1)} %kg_h.1, ...), custom_call_target="tpu_custom_call" | custom-call | tf_op jit(solution)/shard_map/exchange/pallas_call | solution.py:539
  29.4 2.1 %finish.1 = (f32[1,128,2560]{2,1,0:T(8,128)}, f32[1,16,2560]{2,1,0:T(8,128)}, f32[320,128]{1,0:T(8,128)}, f32[320,128]{1,0:T(8,128)}, bf16[320,512]{1,0:T(8,128)...) custom-call(bf16[256,2560]{1,0:T(8,128)(2,1)S(1)} %get-tuple-element, ...), custom_call_target="tpu_custom_call" | custom-call | tf_op jit(solution)/shard_map/finish/pallas_call | solution.py:594

commit v5 on v4

--- a/solution.py
+++ b/solution.py
@@ -298,14 +298,6 @@
         for other in range(2):
             put(summed, summed, 12, (lax.rem(d + j, n_dp), 2 * (1 - x) + other))
 
-    for j in range(1, n_dp):
-        put(nsend.at[0], nrecv.at[d], 1, (lax.rem(d + j, n_dp), s))
-
-    for j in range(1, n_shard):
-        to = (d, lax.rem(s + j, n_shard))
-        put(ukey.at[s], ukey.at[s], 3, to)
-        put(urouter.at[s], urouter.at[s], 9, to)
-
     wait_recv(recv2.at[pl.ds(0, half - 1)], 2)
 
     def factor(which, first):
@@ -354,6 +346,14 @@
         left = stacked(factor(s, 1)[:, :router_rows], factor(mate, 1)[:, :router_rows])
         wait_recv(mrm.at[router_half], 5)
         columns_of(1, left, mrm)
+
+    for j in range(1, n_dp):
+        put(nsend.at[0], nrecv.at[d], 1, (lax.rem(d + j, n_dp), s))
+
+    for j in range(1, n_shard):
+        to = (d, lax.rem(s + j, n_shard))
+        put(ukey.at[s], ukey.at[s], 3, to)
+        put(urouter.at[s], urouter.at[s], 9, to)
 
     wait_recv(recv2.at[pl.ds(0, half)], 12)
 

time: 31.7 us -> 32.1 us (1.013)
  Pallas kernels: 30.9 us -> 31.3 us
    pallas_call x1, Pallas kernels: 28.8 us -> 29.1 us  [fast_body(): pl.pallas_call(functools.partial(exchange_kernel, n_dp, n_shard, rank), o...]
where the time goes in v5:
time: 32.1 us; the launch traced here: 31.9 us
  Pallas kernels  31.3 us (98%)
  between operations  0.66 us (2%)
    pallas_call x1, Pallas kernels, fast_body(): pl.pallas_call(functools.partial(exchange_kernel, n_dp, n_shard, rank), o...  29.1 us
    pallas_call x1, Pallas kernels, fast_body(): pl.pallas_call(functools.partial(finish_kernel, n_dp, n_shard, rank), out...  2.12 us

profile of v5, /device:TPU:0, one launch (start us, length us, event | category | flops | bytes accessed | tf_op | source)
XLA Modules:
  0.0 31.9 jit_solution(4640077264605336719)
XLA Ops:
  0.6 29.1 %exchange.1 = (bf16[256,2560]{1,0:T(8,128)(2,1)S(1)}, bf16[32,2560]{1,0:T(8,128)(2,1)S(1)}, f32[320,128]{1,0:T(8,128)S(1)}, f32[320,128]{1,0:T(8,128)S(1)}, f32[...) custom-call(bf16[1,128,2560]{2,1,0:T(8,128)(2,1)} %kg_h.1, ...), custom_call_target="tpu_custom_call" | custom-call | tf_op jit(solution)/shard_map/exchange/pallas_call | solution.py:539
  29.8 2.1 %finish.1 = (f32[1,128,2560]{2,1,0:T(8,128)}, f32[1,16,2560]{2,1,0:T(8,128)}, f32[320,128]{1,0:T(8,128)}, f32[320,128]{1,0:T(8,128)}, bf16[320,512]{1,0:T(8,128)...) custom-call(bf16[256,2560]{1,0:T(8,128)(2,1)S(1)} %get-tuple-element, ...), custom_call_target="tpu_custom_call" | custom-call | tf_op jit(solution)/shard_map/finish/pallas_call | solution.py:594
